TPU v7x, 256 devices: a whole 4x4x8 slice. The times are simulated.
256 devices in a mesh: chan: 32 (over z, y_hi, core), seg: 4 (over x), win: 2 (over y_lo).
Axes of the slice: x: 4, y: 4 (y_hi: 2, y_lo: 2; y = y_hi * 2 + y_lo), z: 8, core: 2. Of those that a mesh axis runs over, the one named last changes fastest.
Arguments:
- series: bfloat16 [2048, 4096], P('chan', ('win', 'seg')), parts along dimension 1, may hold values from -200 to 200
Outputs:
- xcorr: bfloat16 [130, 2048, 2048], P('win', 'chan', 'seg'), parts along dimension 0
There are 2 independent parts, one for each index of `win`. A program takes and returns all parts, laid end to end along the dimension named above; each array names one. Nothing has to cross between parts.
All inputs are finite; a program needn't handle non-finite values.
Results may differ from a plain program's by a relative error of at most 0.015.
Values may be sent and summed in bfloat16 or wider, within the bound.
No kernel may reach another device: no remote copies, remote signals or barrier semaphores. Data moves between devices by JAX's collectives and lax.ppermute only.
A program may use at most 128 MiB of HBM per device.

v0:
```python
import jax
import jax.numpy as jnp
from jax import lax
from jax.sharding import PartitionSpec as P

HALF_LAG = 32


def lag_products(rows, columns, lags):
    row_len = rows.shape[1]
    col_len = columns.shape[1]
    group = -(-lags // 16)
    turns = -(-lags // group)
    front = turns * group - 1
    padded = jnp.pad(rows, ((0, 0), (front, col_len - row_len)))

    def one_turn(index):
        start = front - index * group - (group - 1)
        block = lax.dynamic_slice_in_dim(padded, start, col_len + group - 1, 1)
        shifted = jnp.stack(
            [block[:, group - 1 - k : group - 1 - k + col_len] for k in range(group)]
        )
        return jnp.einsum("gic,jc->gij", shifted, columns, preferred_element_type=jnp.float32)

    result = lax.map(one_turn, jnp.arange(turns, dtype=jnp.int32))
    return result.reshape((turns * group,) + result.shape[2:])


def on_device(series):
    ch_rows, seg_len = series.shape
    half = HALF_LAG
    lags = 2 * half + 1
    n_seg = lax.axis_size("seg")
    samples = seg_len * n_seg
    channels = ch_rows * lax.axis_size("chan")
    ncols = channels // n_seg
    col_start = lax.axis_index("seg") * ncols
    window = lax.all_gather(series, "seg", axis=1, tiled=True)
    everything = lax.all_gather(window, "chan", axis=0, tiled=True)
    full = everything.astype(jnp.float32)
    energy = jnp.sum(full * full, axis=1) / samples + 1e-06
    scale = lax.rsqrt(energy)
    columns = lax.dynamic_slice_in_dim(everything, col_start, ncols, 0)
    columns = jnp.pad(columns, ((0, 0), (half, half)))
    stacked = lag_products(window, columns, lags)
    row_scale = lax.dynamic_slice_in_dim(scale, lax.axis_index("chan") * ch_rows, ch_rows, 0)
    col_scale = lax.dynamic_slice_in_dim(scale, col_start, ncols, 0)
    result = (
        stacked
        * row_scale[None, :, None]
        * col_scale[None, None, :]
        / jnp.sqrt(jnp.float32(samples))
    )
    return result.astype(jnp.bfloat16)


def solution(mesh):
    placed = (P("chan", ("win", "seg")),)
    return jax.shard_map(
        on_device, mesh=mesh, in_specs=placed, out_specs=P("win", "chan", "seg"), check_vma=False
    )
```

profile of v0, /device:TPU:1, one launch (start us, length us, event | category | flops | bytes accessed | tf_op | source)
XLA Modules:
  0.0 199.8 jit_solution(13141319077814468476)
XLA Ops:
  6.5 12.4 %all_gather.6 = bf16[64,2048]{1,0:T(8,128)(2,1)} all-gather(bf16[64,512]{1,0:T(8,128)(2,1)} %param.3), channel_id=1, replica_groups=mesh['chan'=32,'seg'=4,'win'=2] {'seg'}, dimensions={1}, use_global_device_ids=true | all-gather | bytes 327680 | tf_op jit(solution)/shard_map/all_gather | solution.py:38
  19.0 1.1 pad.8
  20.1 105.2 %all-gather.2.cloned.1.call-done = bf16[2048,2048]{1,0:T(8,128)(2,1)} async-done(((bf16[64,2048]{1,0:T(8,128)(2,1)}), bf16[2048,2048]{1,0:T(8,128)(2,1)}) %all-gather.2.cloned.1.call-update) | async-done | bytes 8388624 | tf_op jit(solution)/shard_map/all_gather | solution.py:39
  125.3 5.1 %multiply_reduce_fusion = f32[2048]{0:T(1024)S(1)} fusion(bf16[2048,2048]{1,0:T(8,128)(2,1)} %all-gather.2.cloned.1.call-done), kind=kLoop, calls=%fused_computation.14 | loop fusion | flops 12580864 | bytes 8396800 | tf_op jit(solution)/shard_map/reduce_sum | solution.py:41
  130.6 1.7 constant_dynamic-slice_fusion
  132.3 2.5 %copy.5 = bf16[512,2048]{0,1:T(8,128)(2,1)} copy(bf16[512,2048]{1,0:T(8,128)(2,1)S(1)} %constant_dynamic-slice_fusion) | data formatting | bytes 4194304
  134.8 1.7 pad.9.clone
  136.5 49.6 %while.14 = (s32[]{:T(128)}, f32[13,5,64,512]{3,2,1,0:T(8,128)}, s32[13]{0:T(128)S(1)}, bf16[64,2176]{1,0:T(8,128)(2,1)S(1)}, bf16[512,2112]{0,1:T(8,128)(2,1)S(...) while((s32[]{:T(128)}, f32[13,5,64,512]{3,2,1,0:T(8,128)}, ...), condition=%wide.region_1.2_spmd, body=%wide.region_0.0_spmd.sunk | while | flops 692060160 | bytes 6947099 | solution.py:25
  136.6 0.6 dynamic_slice.33
  138.6 1.8 fusion.32
  140.4 0.6 dynamic_slice.33
  142.4 1.8 fusion.32
  144.2 0.6 dynamic_slice.33
  146.2 1.8 fusion.32
  148.0 0.6 dynamic_slice.33
  150.1 1.8 fusion.32
  151.8 0.6 dynamic_slice.33
  153.9 1.8 fusion.32
  155.6 0.6 dynamic_slice.33
  157.7 1.8 fusion.32
  159.4 0.6 dynamic_slice.33
  161.4 1.8 fusion.32
  163.2 0.6 dynamic_slice.33
  165.2 1.8 fusion.32
  167.0 0.6 dynamic_slice.33
  169.0 1.8 fusion.32
  172.9 1.8 fusion.32
  176.7 1.8 fusion.32
  180.5 1.8 fusion.32
  182.3 0.6 dynamic_slice.33
  184.3 1.8 fusion.32
  186.1 6.9 %fusion.15 = bf16[65,64,512]{2,1,0:T(8,128)(2,1)} fusion(f32[13,5,64,512]{3,2,1,0:T(8,128)} %get-tuple-element.108, f32[512]{0:T(512)S(1)} %dynamic_slice.30, f32[64]{0:T(128)S(1)} %dynamic_slice.29), kind=kLoop, calls=%fused_computation.18 | loop fusion | flops 8519680 | bytes 12781824 | tf_op jit(solution)/shard_map/convert_element_type | solution.py:54
  (75 shorter events, 11.8 us)
Async XLA Ops:
  6.5 118.8 %all-gather.2.cloned.1.call-start = ((), (), s32[]{:S(2)}) async-start(), calls=%async_computation | async-start | bytes 8650752 | tf_op jit(solution)/shard_map/all_gather | solution.py:39
Sparse Core Ops, SparseCore 0:
  19.1 106.1 all-gather.1
where the time goes:
time: 200 us
  waiting for transfers between devices  105 us (52%)
  local copies, waits for them, and re-layouts  24.6 us (12%)
  matrix products  23.1 us (12%)
  between operations  13.4 us (7%)
  blocking collectives  12.4 us (6%)
  other arithmetic  12 us (6%)
  loops' own time  9.02 us (5%)
    all_gather x1, waiting for transfers between devices, on_device(): everything = lax.all_gather(window, 'chan', axis=0, tiled=True)  105 us
    dot_general x13, matrix products, one_turn(): jnp.einsum('gic,jc->gij', shifted, columns, preferred_element_type=jnp.fl...  23.1 us
    all_gather x1, blocking collectives, on_device(): window = lax.all_gather(series, 'seg', axis=1, tiled=True)  12.4 us
    another operation x1, loops' own time, lag_products(): result = lax.map(one_turn, jnp.arange(turns, dtype=jnp.int32))  9.02 us
    while x52, local copies, waits for them, and re-layouts  7.87 us
    dynamic_slice x13, local copies, waits for them, and re-layouts, lag_products(): result = lax.map(one_turn, jnp.arange(turns, dtype=jnp.int32))  7.57 us
    convert_element_type x1, other arithmetic, on_device(): return result.astype(jnp.bfloat16)  6.87 us
    reduce_sum x1, other arithmetic, on_device(): energy = jnp.sum(full * full, axis=1) / samples + 1e-06  5.08 us
  transfers between devices with their start and end apart: 1, of which 1 were waited for; matrix products, arithmetic and copies ran while one was open for 1% of the time, Pallas kernels for 0%

commit v1 on v0

v1 whole, which is shorter than its diff:
```python
import functools
import itertools

import jax
import jax.numpy as jnp
import numpy as np
from jax import lax
from jax.experimental import pallas as pl
from jax.experimental.pallas import tpu as pltpu
from jax.sharding import PartitionSpec as P

HALF_LAG = 32
LAGS = 2 * HALF_LAG + 1
AXES = ("chan", "seg", "win")
ZS, HS, KS, XS, WS = 8, 2, 2, 4, 2
EDGE = 128
GROUP = 5

DEST = np.array([0, 2, 6, 1, 5, 4, 5, 2, 7, 1, 7, 3, 6, 3, 0, 4, 4, 5, 3, 5, 3, 0, 1, 6, 1, 6, 4, 7, 2, 7, 2, 0, 7, 6, 2, 6, 0, 3, 1, 5, 2, 4, 0, 4, 1, 5, 7, 3, 3, 0, 5, 2, 4, 7, 6, 0, 6, 2, 3, 7, 5, 1, 4, 1, 1, 4, 3, 5, 3, 7, 2, 4, 6, 5, 1, 0, 2, 0, 6, 7, 0, 3, 0, 1, 4, 6, 7, 2, 5, 1, 4, 3, 7, 2, 5, 6, 5, 1, 4, 3, 6, 7, 6, 2, 0, 2, 5, 7, 4, 3, 0, 1, 7, 0, 7, 6, 1, 4, 2, 0, 2, 5, 3, 4, 3, 6, 1, 5]).reshape((4, 2, 4, 2, 2))
FROM = np.array([0, 1, 3, 3, 2, 2, 1, 0, 3, 0, 3, 1, 1, 3, 0, 2, 0, 1, 2, 3, 1, 0, 1, 0, 3, 2, 0, 1, 2, 3, 2, 2, 1, 0, 2, 1, 3, 3, 1, 3, 2, 2, 0, 0, 0, 1, 2, 3, 1, 2, 3, 2, 3, 3, 0, 1, 2, 0, 1, 0, 0, 1, 3, 2, 0, 3, 0, 2, 0, 2, 2, 0, 3, 3, 1, 1, 1, 0, 0, 2, 1, 0, 2, 1, 2, 2, 3, 0, 2, 1, 3, 3, 3, 1, 1, 3, 2, 0, 3, 1, 1, 0, 3, 3, 2, 2, 1, 1, 3, 3, 2, 0, 3, 1, 0, 2, 0, 2, 2, 3, 1, 3, 1, 0, 0, 1, 0, 2]).reshape((4, 8, 2, 2))
FIRST = np.array([0, 1, 1, 1, 1, 0, 0, 0, 0, 0, 0, 1, 1, 1, 1, 0, 1, 0, 0, 0, 1, 1, 0, 1, 0, 1, 1, 1, 0, 0, 0, 1]).reshape((4, 8))


def pairs(target):
    places = itertools.product(range(ZS), range(HS), range(KS), range(XS), range(WS))
    shape = (ZS, HS, KS, XS, WS)
    return [
        (int(np.ravel_multi_index(p, shape)), int(np.ravel_multi_index(target(*p), shape)))
        for p in places
    ]


def send(value, target):
    return lax.ppermute(value, AXES, pairs(target))


def along_x(step):
    return lambda z, h, k, x, w: (z, h, k, (x + step) % XS, w)


def other_y(z, h, k, x, w):
    return z, 1 - h, k, x, w


def other_core(z, h, k, x, w):
    return z, h, 1 - k, x, w


def to_columns(o):
    return lambda z, h, k, x, w: (int(DEST[z // 2, z % 2, x, k, o]), h, k, z // 2, w)


def stack_kernel(where, own, left, right, far, out, scale, rows):
    seg, samples = own.shape[1], own.shape[1] * XS
    x = where[0]

    @pl.when(pl.program_id(0) == 0)
    def _():
        rows[...] = jnp.zeros_like(rows)
        total = jnp.zeros((own.shape[0], 1), jnp.float32)
        for piece, step in ((own, 0), (left, XS - 1), (right, 1), (far, 2)):
            at = pl.multiple_of(EDGE + lax.rem(x + step, XS) * seg, EDGE)
            values = piece[...]
            rows[:, pl.ds(at, seg)] = values
            wide = values.astype(jnp.float32)
            total += jnp.sum(wide * wide, axis=1, keepdims=True)
        norm = lax.rsqrt(total / samples + 1e-06) * (1.0 / np.sqrt(samples))
        scale[...] = jnp.broadcast_to(norm, scale.shape)

    padded = rows[...]
    width = padded.shape[1]
    count = own.shape[0]
    for u in range(GROUP):
        lag = pl.program_id(0) * GROUP + u
        moved = pltpu.roll(padded, lag + (width - EDGE - HALF_LAG), 1)
        out[u * count : (u + 1) * count, :] = moved[:, :samples]


def lag_stack(where, own, left, right, far):
    count, seg = own.shape
    samples = seg * XS
    piece = pl.BlockSpec((count, seg), lambda g, s: (0, 0))
    return pl.pallas_call(
        stack_kernel,
        grid_spec=pltpu.PrefetchScalarGridSpec(
            num_scalar_prefetch=1,
            grid=(LAGS // GROUP,),
            in_specs=[piece] * 4,
            out_specs=[
                pl.BlockSpec((GROUP * count, samples), lambda g, s: (g, 0)),
                pl.BlockSpec((count, EDGE), lambda g, s: (0, 0)),
            ],
            scratch_shapes=[pltpu.VMEM((count, samples + 2 * EDGE), jnp.bfloat16)],
        ),
        out_shape=[
            jax.ShapeDtypeStruct((LAGS * count, samples), jnp.bfloat16),
            jax.ShapeDtypeStruct((count, EDGE), jnp.float32),
        ],
        compiler_params=pltpu.CompilerParams(vmem_limit_bytes=40 * 2**20),
    )(where, own, left, right, far)


def match_kernel(group, where, stack, row_scale, *refs):
    pieces, (out, columns, col_scale) = refs[:4], refs[-3:]
    count, seg = pieces[0].shape[1:]
    samples = seg * XS
    width = columns.shape[0]

    @pl.when(pl.program_id(0) == 0)
    def _():
        for n, piece in enumerate(pieces):
            row = pl.multiple_of(where[1 + n] * count, count)
            for q, step in enumerate((0, XS - 1, 1, 2)):
                at = pl.multiple_of(lax.rem(where[5 + n] + step, XS) * seg, EDGE)
                columns[pl.ds(row, count), pl.ds(at, seg)] = piece[q]
        wide = columns[...].astype(jnp.float32)
        total = jnp.sum(wide * wide, axis=1, keepdims=True)
        norm = lax.rsqrt(total / samples + 1e-06)
        col_scale[...] = jnp.broadcast_to(norm, (width, EDGE)).T[:8]

    products = lax.dot_general(
        stack[...], columns[...], (((1,), (1,)), ((), ())), preferred_element_type=jnp.float32
    )
    scaled = products.reshape(group, count, width) * row_scale[:, :1][None] * col_scale[:1][None]
    out[...] = scaled.astype(jnp.bfloat16)


def match(where, stack, row_scale, pieces, result, columns):
    count, seg = pieces[0].shape[1:]
    samples = seg * XS
    group = 13
    width = 4 * count
    whole = pl.BlockSpec(pieces[0].shape, lambda g, s: (0, 0, 0))
    before = [] if result is None else [result]
    return pl.pallas_call(
        functools.partial(match_kernel, group),
        grid_spec=pltpu.PrefetchScalarGridSpec(
            num_scalar_prefetch=1,
            grid=(LAGS // group,),
            in_specs=[
                pl.BlockSpec((group * count, samples), lambda g, s: (g, 0)),
                pl.BlockSpec((count, EDGE), lambda g, s: (0, 0)),
            ]
            + [whole] * 4
            + [pl.BlockSpec(memory_space=pl.ANY)] * len(before),
            out_specs=pl.BlockSpec((group, count, width), lambda g, s: (g, 0, s[0])),
            scratch_shapes=[
                pltpu.VMEM((width, samples), jnp.bfloat16),
                pltpu.VMEM((8, width), jnp.float32),
            ],
        ),
        out_shape=jax.ShapeDtypeStruct((LAGS, count, columns), jnp.bfloat16),
        input_output_aliases={7: 0} if before else {},
        compiler_params=pltpu.CompilerParams(vmem_limit_bytes=50 * 2**20),
        cost_estimate=pl.CostEstimate(
            flops=2 * LAGS * count * width * samples,
            bytes_accessed=2 * LAGS * count * (samples + width),
            transcendentals=0,
        ),
    )(where, stack, row_scale, *pieces, *before)


def on_device(series):
    count, seg = series.shape
    x = lax.axis_index("seg")
    chan = lax.axis_index("chan")
    z, h, k = chan // 4, chan // 2 % 2, chan % 2
    source = jnp.asarray(FROM, jnp.int32)[x, z]
    first = jnp.asarray(FIRST, jnp.int32)[x, z]

    left = send(series, along_x(1))
    right = send(series, along_x(-1))
    far = send(series, along_x(2))
    window = jnp.stack([series, left, right, far])
    stack, row_scale = lag_stack(jnp.stack([x]), series, left, right, far)

    result = None
    halves = []
    for o in range(2):
        mine = send(window, to_columns(o))
        beside = send(mine, other_y)
        halves.append((mine, beside, send(mine, other_core), send(beside, other_core)))
    for o, pieces in enumerate(halves):
        part = first if o == 0 else 1 - first
        places = [part]
        places += [h * 2 + k, (1 - h) * 2 + k, h * 2 + 1 - k, (1 - h) * 2 + 1 - k]
        places += [source[k, o], source[k, o], source[1 - k, o], source[1 - k, o]]
        where = jnp.stack([jnp.asarray(p, jnp.int32) for p in places])
        result = match(where, stack, row_scale, pieces, result, 8 * count)
    return result


def solution(mesh):
    placed = (P("chan", ("win", "seg")),)
    return jax.shard_map(
        on_device, mesh=mesh, in_specs=placed, out_specs=P("win", "chan", "seg"), check_vma=False
    )
```

time: 200 us -> 87.9 us (0.44)
  the two profiles are of different devices: /device:TPU:1 before, /device:TPU:233 now
where the time goes in v1:
time: 87.9 us; the launch traced here: 87.4 us
  Pallas kernels  34.1 us (39%)
  waiting for transfers between devices  22.6 us (26%)
  starting transfers between devices  19.7 us (22%)
  local copies, waits for them, and re-layouts  9.59 us (11%)
    pallas_call x2, Pallas kernels, match(): pl.pallas_call(functools.partial(match_kernel, group), grid_spec=pltpu.Pr...  22.8 us
    ppermute x11, waiting for transfers between devices, send(): return lax.ppermute(value, AXES, pairs(target))  22.6 us
    ppermute x11, starting transfers between devices, send(): return lax.ppermute(value, AXES, pairs(target))  19.7 us
    pallas_call x1, Pallas kernels, lag_stack(): pl.pallas_call(stack_kernel, grid_spec=pltpu.PrefetchScalarGridSpec(num_s...  11.3 us
    another operation x2, local copies, waits for them, and re-layouts, on_device(): where = jnp.stack([jnp.asarray(p, jnp.int32) for p in places])  5.98 us
  transfers between devices with their start and end apart: 11, of which 5 were waited for; matrix products, arithmetic and copies ran while one was open for 10% of the time, Pallas kernels for 26%

profile of v1, /device:TPU:233, one launch (start us, length us, event | category | flops | bytes accessed | tf_op | source)
XLA Modules:
  0.0 87.4 jit_solution(9417359160800383614)
XLA Ops:
  0.0 2.7 %collective-permute-start.2 = (bf16[64,512]{1,0:T(8,128)(2,1)}, bf16[64,512]{1,0:T(8,128)(2,1)S(1)}, u32[]{:S(2)}, u32[]{:S(2)}) collective-permute-start(bf16[64,512]{1,0:T(8,128)(2,1)} %own.1), channel_id=1, source_target_pairs={{0,4},{1,5},{2,6},{3,7},{4,0},{5,1},{6,2},{7,3},{8,12},{9,13},{10,... | collective-permute-start | bytes 196616 | tf_op jit(solution)/shard_map/ppermute | solution.py:34
  2.7 0.9 collective-permute-start.1
  3.6 0.6 collective-permute-start
  4.2 0.6 collective-permute-done.2.far
  4.8 1.9 %collective-permute-done.1.right = bf16[64,512]{1,0:T(8,128)(2,1)S(1)} collective-permute-done((bf16[64,512]{1,0:T(8,128)(2,1)}, bf16[64,512]{1,0:T(8,128)(2,1)S(1)}, u32[]{:S(2)}, u32[]{:S(2)}) %collective-permute-start.1) | collective-permute-done | bytes 65568 | tf_op jit(solution)/shard_map/ppermute | solution.py:34
  6.8 1.4 %collective-permute-done.left = bf16[64,512]{1,0:T(8,128)(2,1)S(1)} collective-permute-done((bf16[64,512]{1,0:T(8,128)(2,1)}, bf16[64,512]{1,0:T(8,128)(2,1)S(1)}, u32[]{:S(2)}, u32[]{:S(2)}) %collective-permute-start) | collective-permute-done | bytes 65568 | tf_op jit(solution)/shard_map/ppermute | solution.py:34
  8.1 0.9 %pad_maximum_fusion = bf16[4,64,512]{2,1,0:T(8,128)(2,1)S(1)} fusion(bf16[1,64,512]{2,1,0:T(8,128)(2,1)S(1)} %bitcast.16, bf16[1,64,512]{2,1,0:T(8,128)(2,1)S(1)} %bitcast.17, bf16[1,64,512]{2,1,0:T(8,128)(2,1)S(1)} %bitcast.18, bf16[1,64,512]{2,1,0:T(8,128)(2,1)} %bitcast.15), kind=kLoop, calls=%fused_computation | loop fusion | flops 393216 | bytes 524288 | tf_op jit(solution)/shard_map/stack | solution.py:174
  9.0 2.6 %collective-permute-start.7 = (bf16[4,64,512]{2,1,0:T(8,128)(2,1)S(1)}, bf16[4,64,512]{2,1,0:T(8,128)(2,1)S(1)}, u32[]{:S(2)}, u32[]{:S(2)}) collective-permute-start(bf16[4,64,512]{2,1,0:T(8,128)(2,1)S(1)} %pad_maximum_fusion), channel_id=1, source_target_pairs={{0,0},{1,1},{2,160},{3,161},{4,224},{5,225},{6,192},{7,193},{8,200... | collective-permute-start | bytes 786440 | tf_op jit(solution)/shard_map/ppermute | solution.py:34
  11.6 0.5 collective-permute-start.3
  12.2 17.4 %collective-permute-done.7.refs_0_ = bf16[4,64,512]{2,1,0:T(8,128)(2,1)S(1)} collective-permute-done((bf16[4,64,512]{2,1,0:T(8,128)(2,1)S(1)}, bf16[4,64,512]{2,1,0:T(8,128)(2,1)S(1)}, u32[]{:S(2)}, u32[]{:S(2)}) %collective-permute-start.7) | collective-permute-done | bytes 262176 | tf_op jit(solution)/shard_map/ppermute | solution.py:34
  29.6 2.0 %collective-permute-start.8 = (bf16[4,64,512]{2,1,0:T(8,128)(2,1)S(1)}, bf16[4,64,512]{2,1,0:T(8,128)(2,1)S(1)}, u32[]{:S(2)}, u32[]{:S(2)}) collective-permute-start(bf16[4,64,512]{2,1,0:T(8,128)(2,1)S(1)} %collective-permute-done.7.refs_0_), channel_id=1, source_target_pairs={{0,16},{1,17},{2,18},{3,19},{4,20},{5,21},{6,22},{7,23},{8,24},{9,... | collective-permute-start | bytes 786440 | tf_op jit(solution)/shard_map/ppermute | solution.py:34
  31.6 0.0 collective-permute-done.3.refs_0_
  31.6 1.0 %collective-permute-start.4 = (bf16[4,64,512]{2,1,0:T(8,128)(2,1)S(1)}, bf16[4,64,512]{2,1,0:T(8,128)(2,1)S(1)}, u32[]{:S(2)}, u32[]{:S(2)}) collective-permute-start(bf16[4,64,512]{2,1,0:T(8,128)(2,1)S(1)} %collective-permute-done.3.refs_0_), channel_id=1, source_target_pairs={{0,16},{1,17},{2,18},{3,19},{4,20},{5,21},{6,22},{7,23},{8,24},{9,... | collective-permute-start | bytes 786440 | tf_op jit(solution)/shard_map/ppermute | solution.py:34
  32.5 2.8 %collective-permute-start.9 = (bf16[4,64,512]{2,1,0:T(8,128)(2,1)S(1)}, bf16[4,64,512]{2,1,0:T(8,128)(2,1)S(1)}, u32[]{:S(2)}, u32[]{:S(2)}) collective-permute-start(bf16[4,64,512]{2,1,0:T(8,128)(2,1)S(1)} %collective-permute-done.7.refs_0_), channel_id=1, source_target_pairs={{0,8},{1,9},{2,10},{3,11},{4,12},{5,13},{6,14},{7,15},{8,0},{9,1},... | collective-permute-start | bytes 786440 | tf_op jit(solution)/shard_map/ppermute | solution.py:34
  35.4 1.2 %collective-permute-done.8.refs_1_ = bf16[4,64,512]{2,1,0:T(8,128)(2,1)S(1)} collective-permute-done((bf16[4,64,512]{2,1,0:T(8,128)(2,1)S(1)}, bf16[4,64,512]{2,1,0:T(8,128)(2,1)S(1)}, u32[]{:S(2)}, u32[]{:S(2)}) %collective-permute-start.8) | collective-permute-done | bytes 262176 | tf_op jit(solution)/shard_map/ppermute | solution.py:34
  36.6 6.0 %collective-permute-start.10 = (bf16[4,64,512]{2,1,0:T(8,128)(2,1)S(1)}, bf16[4,64,512]{2,1,0:T(8,128)(2,1)S(1)}, u32[]{:S(2)}, u32[]{:S(2)}) collective-permute-start(bf16[4,64,512]{2,1,0:T(8,128)(2,1)S(1)} %collective-permute-done.8.refs_1_), channel_id=1, source_target_pairs={{0,8},{1,9},{2,10},{3,11},{4,12},{5,13},{6,14},{7,15},{8,0},{9,1},... | collective-permute-start | bytes 786440 | tf_op jit(solution)/shard_map/ppermute | solution.py:34
  42.6 1.3 %dynamic_slice.20 = s32[1,1]{1,0:T(1,128)} dynamic-slice(s32[4,8]{1,0:T(4,128)} %constant.155.clone, s32[]{:T(128)S(6)} %select_n.46, s32[]{:T(128)S(6)} %select_n.48), dynamic_slice_sizes={1,1} | dynamic-slice | bytes 12 | tf_op jit(solution)/shard_map/dynamic_slice | solution.py:169
  44.4 1.5 %constant_dynamic-slice_fusion.2 = (s32[1,1,1,1]{3,2,1,0:T(1,128)}, s32[1,1,1,1]{3,2,1,0:T(1,128)}, s32[1,1,1,1]{3,2,1,0:T(1,128)}, s32[1,1,1,1]{3,2,1,0:T(1,128)}) fusion(s32[4,8,2,2]{3,2,1,0:T(2,128)} %constant.154.clone, s32[]{:T(128)S(6)} %select_n.52, s32[]{:T(128)S(6)} %select_n.53, s32[]{:T(128)S(6)} %select_n.57, s32[]{:T(128)S(6)} %select_n.55), kind=kLoop, calls=%fused_computation.3 | loop fusion | bytes 48 | tf_op jit(solution)/shard_map/dynamic_slice | solution.py:187
  45.9 3.1 %stack.55.where = s32[9]{0:T(128)S(1)} concatenate(s32[1]{0:T(128)} %bitcast.12, s32[1]{0:T(128)} %bitcast.1, s32[1]{0:T(128)} %bitcast.2, s32[1]{0:T(128)} %bitcast.3, s32[1]{0:T(128)} %bitcast.4, s32[1]{0:T(128)} %bitcast.13, s32[1]{0:T(128)} %bitcast.13, s32[1]{0:T(128)} %bitcast.14, s32[1]{0:T(128)} %bitcast.14), dimensions={0} | concatenate | bytes 72 | tf_op jit(solution)/shard_map/stack | solution.py:188
  49.1 2.8 %stack.48.where = s32[9]{0:T(128)S(1)} concatenate(s32[1]{0:T(128)} %bitcast, s32[1]{0:T(128)} %bitcast.1, s32[1]{0:T(128)} %bitcast.2, s32[1]{0:T(128)} %bitcast.3, s32[1]{0:T(128)} %bitcast.4, s32[1]{0:T(128)} %bitcast.5, s32[1]{0:T(128)} %bitcast.5, s32[1]{0:T(128)} %bitcast.6, s32[1]{0:T(128)} %bitcast.6), dimensions={0} | concatenate | bytes 72 | tf_op jit(solution)/shard_map/stack | solution.py:188
  51.9 0.0 copy-start
  51.9 0.8 copy-done
  52.7 11.3 %shard_map.37 = (bf16[4160,2048]{1,0:T(8,128)(2,1)}, f32[64,128]{1,0:T(8,128)S(1)}) custom-call(s32[1]{0:T(128)} %bitcast.7.where, bf16[64,512]{1,0:T(8,128)(2,1)S(1)} %copy-done, bf16[64,512]{1,0:T(8,128)(2,1)S(1)} %collective-permute-done.left, bf16[64,512]{1,0:T(8,128)(2,1)S(1)} %collective-permute-done.1.right, ...), custom_call_target="tpu_custom_call" | custom-call | tf_op jit(solution)/shard_map/pallas_call | solution.py:83
  64.1 0.0 collective-permute-start.5
  64.1 0.0 collective-permute-done.4.refs_1_
  64.1 0.5 collective-permute-start.6
  64.6 0.0 collective-permute-done.9.refs_2_
  64.6 0.0 collective-permute-done.10.refs_3_
  64.6 11.4 %shard_map.38.refs_4_ = bf16[65,64,512]{2,1,0:T(8,128)(2,1)} custom-call(s32[9]{0:T(128)S(1)} %stack.55.where, bf16[4160,2048]{1,0:T(8,128)(2,1)} %get-tuple-element.7.stack, f32[64,128]{1,0:T(8,128)S(1)} %get-tuple-element.8.row_scale, bf16[4,64,512]{2,1,0:T(8,128)(2,1)S(1)} %collective-permute-done.7.refs_0_, ...), custom_call_target="tpu_custom_call" | custom-call | flops 4362076160 | bytes 19169280 | tf_op jit(solution)/shard_map/pallas_call | solution.py:135
  76.0 0.0 collective-permute-done.5.refs_2_
  76.0 0.0 collective-permute-done.6.refs_3_
  76.0 11.4 %shard_map.39 = bf16[65,64,512]{2,1,0:T(8,128)(2,1)} custom-call(s32[9]{0:T(128)S(1)} %stack.48.where, bf16[4160,2048]{1,0:T(8,128)(2,1)} %get-tuple-element.7.stack, f32[64,128]{1,0:T(8,128)S(1)} %get-tuple-element.8.row_scale, bf16[4,64,512]{2,1,0:T(8,128)(2,1)S(1)} %collective-permute-done.3.refs_0_, ...), custom_call_target="tpu_custom_call", output_to_operand_aliasing={{}: (7, {})} | custom-call | flops 4362076160 | bytes 19169280 | tf_op jit(solution)/shard_map/pallas_call | solution.py:135
Async XLA Ops:
  0.0 4.8 %collective-permute-start.2 = (bf16[64,512]{1,0:T(8,128)(2,1)}, bf16[64,512]{1,0:T(8,128)(2,1)S(1)}, u32[]{:S(2)}, u32[]{:S(2)}) collective-permute-start(bf16[64,512]{1,0:T(8,128)(2,1)} %own.1), channel_id=1, source_target_pairs={{0,4},{1,5},{2,6},{3,7},{4,0},{5,1},{6,2},{7,3},{8,12},{9,13},{10,... | collective-permute-start | bytes 196616 | tf_op jit(solution)/shard_map/ppermute | solution.py:34
  2.7 4.0 %collective-permute-start.1 = (bf16[64,512]{1,0:T(8,128)(2,1)}, bf16[64,512]{1,0:T(8,128)(2,1)S(1)}, u32[]{:S(2)}, u32[]{:S(2)}) collective-permute-start(bf16[64,512]{1,0:T(8,128)(2,1)} %own.1), channel_id=1, source_target_pairs={{0,6},{1,7},{2,0},{3,1},{4,2},{5,3},{6,4},{7,5},{8,14},{9,15},{10,... | collective-permute-start | bytes 196616 | tf_op jit(solution)/shard_map/ppermute | solution.py:34
  3.6 4.5 %collective-permute-start = (bf16[64,512]{1,0:T(8,128)(2,1)}, bf16[64,512]{1,0:T(8,128)(2,1)S(1)}, u32[]{:S(2)}, u32[]{:S(2)}) collective-permute-start(bf16[64,512]{1,0:T(8,128)(2,1)} %own.1), channel_id=1, source_target_pairs={{0,2},{1,3},{2,4},{3,5},{4,6},{5,7},{6,0},{7,1},{8,10},{9,11},{10,... | collective-permute-start | bytes 196616 | tf_op jit(solution)/shard_map/ppermute | solution.py:34
  9.0 20.5 %collective-permute-start.7 = (bf16[4,64,512]{2,1,0:T(8,128)(2,1)S(1)}, bf16[4,64,512]{2,1,0:T(8,128)(2,1)S(1)}, u32[]{:S(2)}, u32[]{:S(2)}) collective-permute-start(bf16[4,64,512]{2,1,0:T(8,128)(2,1)S(1)} %pad_maximum_fusion), channel_id=1, source_target_pairs={{0,0},{1,1},{2,160},{3,161},{4,224},{5,225},{6,192},{7,193},{8,200... | collective-permute-start | bytes 786440 | tf_op jit(solution)/shard_map/ppermute | solution.py:34
  11.6 19.9 %collective-permute-start.3 = (bf16[4,64,512]{2,1,0:T(8,128)(2,1)S(1)}, bf16[4,64,512]{2,1,0:T(8,128)(2,1)S(1)}, u32[]{:S(2)}, u32[]{:S(2)}) collective-permute-start(bf16[4,64,512]{2,1,0:T(8,128)(2,1)S(1)} %pad_maximum_fusion), channel_id=1, source_target_pairs={{0,64},{1,65},{2,128},{3,129},{4,32},{5,33},{6,96},{7,97},{8,40},{... | collective-permute-start | bytes 786440 | tf_op jit(solution)/shard_map/ppermute | solution.py:34
  29.6 7.0 %collective-permute-start.8 = (bf16[4,64,512]{2,1,0:T(8,128)(2,1)S(1)}, bf16[4,64,512]{2,1,0:T(8,128)(2,1)S(1)}, u32[]{:S(2)}, u32[]{:S(2)}) collective-permute-start(bf16[4,64,512]{2,1,0:T(8,128)(2,1)S(1)} %collective-permute-done.7.refs_0_), channel_id=1, source_target_pairs={{0,16},{1,17},{2,18},{3,19},{4,20},{5,21},{6,22},{7,23},{8,24},{9,... | collective-permute-start | bytes 786440 | tf_op jit(solution)/shard_map/ppermute | solution.py:34
  31.6 32.5 %collective-permute-start.4 = (bf16[4,64,512]{2,1,0:T(8,128)(2,1)S(1)}, bf16[4,64,512]{2,1,0:T(8,128)(2,1)S(1)}, u32[]{:S(2)}, u32[]{:S(2)}) collective-permute-start(bf16[4,64,512]{2,1,0:T(8,128)(2,1)S(1)} %collective-permute-done.3.refs_0_), channel_id=1, source_target_pairs={{0,16},{1,17},{2,18},{3,19},{4,20},{5,21},{6,22},{7,23},{8,24},{9,... | collective-permute-start | bytes 786440 | tf_op jit(solution)/shard_map/ppermute | solution.py:34
  32.5 32.0 %collective-permute-start.9 = (bf16[4,64,512]{2,1,0:T(8,128)(2,1)S(1)}, bf16[4,64,512]{2,1,0:T(8,128)(2,1)S(1)}, u32[]{:S(2)}, u32[]{:S(2)}) collective-permute-start(bf16[4,64,512]{2,1,0:T(8,128)(2,1)S(1)} %collective-permute-done.7.refs_0_), channel_id=1, source_target_pairs={{0,8},{1,9},{2,10},{3,11},{4,12},{5,13},{6,14},{7,15},{8,0},{9,1},... | collective-permute-start | bytes 786440 | tf_op jit(solution)/shard_map/ppermute | solution.py:34
  36.6 28.0 %collective-permute-start.10 = (bf16[4,64,512]{2,1,0:T(8,128)(2,1)S(1)}, bf16[4,64,512]{2,1,0:T(8,128)(2,1)S(1)}, u32[]{:S(2)}, u32[]{:S(2)}) collective-permute-start(bf16[4,64,512]{2,1,0:T(8,128)(2,1)S(1)} %collective-permute-done.8.refs_1_), channel_id=1, source_target_pairs={{0,8},{1,9},{2,10},{3,11},{4,12},{5,13},{6,14},{7,15},{8,0},{9,1},... | collective-permute-start | bytes 786440 | tf_op jit(solution)/shard_map/ppermute | solution.py:34
  51.9 0.8 copy-start
  64.1 11.9 %collective-permute-start.5 = (bf16[4,64,512]{2,1,0:T(8,128)(2,1)S(1)}, bf16[4,64,512]{2,1,0:T(8,128)(2,1)S(1)}, u32[]{:S(2)}, u32[]{:S(2)}) collective-permute-start(bf16[4,64,512]{2,1,0:T(8,128)(2,1)S(1)} %collective-permute-done.3.refs_0_), channel_id=1, source_target_pairs={{0,8},{1,9},{2,10},{3,11},{4,12},{5,13},{6,14},{7,15},{8,0},{9,1},... | collective-permute-start | bytes 786440 | tf_op jit(solution)/shard_map/ppermute | solution.py:34
  64.1 11.9 %collective-permute-start.6 = (bf16[4,64,512]{2,1,0:T(8,128)(2,1)S(1)}, bf16[4,64,512]{2,1,0:T(8,128)(2,1)S(1)}, u32[]{:S(2)}, u32[]{:S(2)}) collective-permute-start(bf16[4,64,512]{2,1,0:T(8,128)(2,1)S(1)} %collective-permute-done.4.refs_1_), channel_id=1, source_target_pairs={{0,8},{1,9},{2,10},{3,11},{4,12},{5,13},{6,14},{7,15},{8,0},{9,1},... | collective-permute-start | bytes 786440 | tf_op jit(solution)/shard_map/ppermute | solution.py:34

commit v2 on v0

v2 whole, which is shorter than its diff:
```python
import functools
import itertools

import jax
import jax.numpy as jnp
import numpy as np
from jax import lax
from jax.experimental import pallas as pl
from jax.experimental.pallas import tpu as pltpu
from jax.sharding import PartitionSpec as P

HALF_LAG = 32
LAGS = 2 * HALF_LAG + 1
AXES = ("chan", "seg", "win")
ZS, HS, KS, XS, WS = 8, 2, 2, 4, 2
EDGE = 128

GROUP = 13
PHASES = 4
REACH = HALF_LAG // PHASES

DEST = np.array([0, 2, 6, 1, 5, 4, 5, 2, 7, 1, 7, 3, 6, 3, 0, 4, 4, 5, 3, 5, 3, 0, 1, 6, 1, 6, 4, 7, 2, 7, 2, 0, 7, 6, 2, 6, 0, 3, 1, 5, 2, 4, 0, 4, 1, 5, 7, 3, 3, 0, 5, 2, 4, 7, 6, 0, 6, 2, 3, 7, 5, 1, 4, 1, 1, 4, 3, 5, 3, 7, 2, 4, 6, 5, 1, 0, 2, 0, 6, 7, 0, 3, 0, 1, 4, 6, 7, 2, 5, 1, 4, 3, 7, 2, 5, 6, 5, 1, 4, 3, 6, 7, 6, 2, 0, 2, 5, 7, 4, 3, 0, 1, 7, 0, 7, 6, 1, 4, 2, 0, 2, 5, 3, 4, 3, 6, 1, 5]).reshape((4, 2, 4, 2, 2))
FIRST_BITS = -1900972002


def pairs(target):
    places = itertools.product(range(ZS), range(HS), range(KS), range(XS), range(WS))
    shape = (ZS, HS, KS, XS, WS)
    return [
        (int(np.ravel_multi_index(p, shape)), int(np.ravel_multi_index(target(*p), shape)))
        for p in places
    ]


def send(value, target):
    return lax.ppermute(value, AXES, pairs(target))


def along_x(step):
    return lambda z, h, k, x, w: (z, h, k, (x + step) % XS, w)


def other_y(z, h, k, x, w):
    return z, 1 - h, k, x, w


def other_core(z, h, k, x, w):
    return z, h, 1 - k, x, w


def to_columns(o):
    return lambda z, h, k, x, w: (int(DEST[z // 2, z % 2, x, k, o]), h, k, z // 2, w)


def part_of(me, o):
    bit = lax.rem(me, XS) * ZS + me // (XS * KS * HS)
    first = lax.shift_right_logical(jnp.int32(FIRST_BITS), bit.astype(jnp.int32)) & 1
    return first if o == 0 else 1 - first


def window_kernel(me, own, left, right, far, out):
    x = lax.rem(me[0], XS)
    seg = own.shape[1]
    sample = lax.broadcasted_iota(jnp.int32, (seg, seg), 0)
    place = lax.broadcasted_iota(jnp.int32, (seg, seg), 1)
    move = lax.rem(sample, PHASES) * EDGE + sample // PHASES == place
    move = jnp.where(move, 1.0, 0.0).astype(jnp.bfloat16)
    for piece, step in ((own, 0), (left, XS - 1), (right, 1), (far, 2)):
        values = jnp.dot(piece[...], move, preferred_element_type=jnp.float32)
        out[pl.ds(lax.rem(x + step, XS), 1)] = values.astype(jnp.bfloat16)[None]


def whole_window(me, own, left, right, far):
    return pl.pallas_call(
        window_kernel,
        in_specs=[pl.BlockSpec(memory_space=pltpu.SMEM)]
        + [pl.BlockSpec(memory_space=pltpu.VMEM)] * 4,
        out_specs=pl.BlockSpec(memory_space=pltpu.VMEM),
        out_shape=jax.ShapeDtypeStruct((XS,) + own.shape, own.dtype),
        compiler_params=pltpu.CompilerParams(vmem_limit_bytes=16 * 2**20),
    )(me, own, left, right, far)


def shift_kernel(window, out, scale):
    count, seg = window.shape[1:]
    edge = jnp.zeros((count, EDGE), jnp.bfloat16)
    total = jnp.zeros((count, 1), jnp.float32)
    for g in range(XS):
        wide = window[g].astype(jnp.float32)
        total += jnp.sum(wide * wide, axis=1, keepdims=True)
    samples = seg * XS
    norm = lax.rsqrt(total / samples + 1e-06) * (1.0 / np.sqrt(samples))
    scale[...] = jnp.broadcast_to(norm, scale.shape)
    for j in range(PHASES):
        tiles = [window[g, :, j * EDGE : (j + 1) * EDGE] for g in range(XS)]
        row = jnp.concatenate([edge] + tiles + [edge], axis=1)
        for o in range(2 * REACH + 1):
            moved = pltpu.roll(row, (REACH - o) % row.shape[1], 1)
            at = (PHASES * o + j) * EDGE
            for g in range(XS):
                out[g, :, at : at + EDGE] = moved[:, (g + 1) * EDGE : (g + 2) * EDGE]


def shifts(window):
    count, seg = window.shape[1:]
    width = (2 * REACH + 1) * PHASES * EDGE
    return pl.pallas_call(
        shift_kernel,
        in_specs=[pl.BlockSpec(memory_space=pltpu.VMEM)],
        out_specs=[pl.BlockSpec(memory_space=pltpu.VMEM)] * 2,
        out_shape=[
            jax.ShapeDtypeStruct((XS, count, width), jnp.bfloat16),
            jax.ShapeDtypeStruct((count, EDGE), jnp.float32),
        ],
        compiler_params=pltpu.CompilerParams(vmem_limit_bytes=16 * 2**20),
        cost_estimate=pl.CostEstimate(
            flops=0, bytes_accessed=8 * XS * count * width, transcendentals=0
        ),
    )(window)


def match_kernel(me, moved, row_scale, *refs):
    pieces, (out, columns, col_scale) = refs[:4], refs[-3:]
    count, seg = pieces[0].shape[1:]
    samples = seg * XS
    width = columns.shape[1]

    @pl.when(pl.program_id(0) == 0)
    def _():
        h, k = lax.rem(me[0] // (XS * KS), HS), lax.rem(me[0] // XS, KS)
        for piece, at in zip(pieces, (h * 2 + k, 2 - h * 2 + k, h * 2 + 1 - k, 3 - h * 2 - k)):
            row = pl.multiple_of(at * count, count)
            for g in range(XS):
                columns[g, pl.ds(row, count)] = piece[g]
        total = jnp.zeros((width, 1), jnp.float32)
        for g in range(XS):
            wide = columns[g].astype(jnp.float32)
            total += jnp.sum(wide * wide, axis=1, keepdims=True)
        norm = lax.rsqrt(total / samples + 1e-06)
        col_scale[...] = jnp.broadcast_to(norm, (width, EDGE)).T[:8]

    last = 2 * HALF_LAG - pl.program_id(0) * GROUP
    products = jnp.zeros((GROUP * count, width), jnp.float32)
    for g in range(XS):
        rows = jnp.concatenate(
            [
                moved[g, :, pl.ds(pl.multiple_of((last - u) * EDGE, EDGE), seg)]
                for u in range(GROUP)
            ],
            axis=0,
        )
        products += lax.dot_general(
            rows, columns[g], (((1,), (1,)), ((), ())), preferred_element_type=jnp.float32
        )
    scaled = products.reshape(GROUP, count, width) * row_scale[:, :1][None] * col_scale[:1][None]
    out[...] = scaled.astype(jnp.bfloat16)


def match(me, o, moved, row_scale, pieces, result, columns):
    count, seg = pieces[0].shape[1:]
    samples = seg * XS
    width = 4 * count
    inside = pl.BlockSpec(memory_space=pltpu.VMEM)
    before = [] if result is None else [result]
    return pl.pallas_call(
        match_kernel,
        grid_spec=pltpu.PrefetchScalarGridSpec(
            num_scalar_prefetch=1,
            grid=(LAGS // GROUP,),
            in_specs=[inside] * 6 + [pl.BlockSpec(memory_space=pl.ANY)] * len(before),
            out_specs=pl.BlockSpec((GROUP, count, width), lambda g, me: (g, 0, part_of(me[0], o))),
            scratch_shapes=[
                pltpu.VMEM((XS, width, seg), jnp.bfloat16),
                pltpu.VMEM((8, width), jnp.float32),
            ],
        ),
        out_shape=jax.ShapeDtypeStruct((LAGS, count, columns), jnp.bfloat16),
        input_output_aliases={7: 0} if before else {},
        compiler_params=pltpu.CompilerParams(vmem_limit_bytes=32 * 2**20),
        cost_estimate=pl.CostEstimate(
            flops=2 * LAGS * count * width * samples,
            bytes_accessed=2 * LAGS * count * width,
            transcendentals=0,
        ),
    )(me, moved, row_scale, *pieces, *before)


def on_device(series):
    count = series.shape[0]
    me = (lax.axis_index("chan") * XS + lax.axis_index("seg")).reshape(1)
    left = send(series, along_x(1))
    right = send(series, along_x(-1))
    far = send(series, along_x(2))
    window = whole_window(me, series, left, right, far)
    moved, row_scale = shifts(window)
    halves = []
    for o in range(2):
        mine = send(window, to_columns(o))
        beside = send(mine, other_y)
        halves.append((mine, beside, send(mine, other_core), send(beside, other_core)))
    result = None
    for o, pieces in enumerate(halves):
        result = match(me, o, moved, row_scale, pieces, result, 8 * count)
    return result


def solution(mesh):
    placed = (P("chan", ("win", "seg")),)
    return jax.shard_map(
        on_device, mesh=mesh, in_specs=placed, out_specs=P("win", "chan", "seg"), check_vma=False
    )
```

time: 200 us -> 59.2 us (0.30)
  the two profiles are of different devices: /device:TPU:1 before, /device:TPU:225 now
where the time goes in v2:
time: 59.2 us; the launch traced here: 59.1 us
  starting transfers between devices  23.2 us (39%)
  waiting for transfers between devices  19.8 us (33%)
  Pallas kernels  15.2 us (26%)
  local copies, waits for them, and re-layouts  0.84 us (1%)
    ppermute x11, starting transfers between devices, send(): return lax.ppermute(value, AXES, pairs(target))  23.2 us
    ppermute x11, waiting for transfers between devices, send(): return lax.ppermute(value, AXES, pairs(target))  19.8 us
    pallas_call x2, Pallas kernels, match(): pl.pallas_call(match_kernel, grid_spec=pltpu.PrefetchScalarGridSpec(num_s...  13.4 us
    pallas_call x1, Pallas kernels, shifts(): pl.pallas_call(shift_kernel, in_specs=[pl.BlockSpec(memory_space=pltpu.VM...  1.22 us
  transfers between devices with their start and end apart: 11, of which 4 were waited for; matrix products, arithmetic and copies ran while one was open for 0% of the time, Pallas kernels for 13%

profile of v2, /device:TPU:225, one launch (start us, length us, event | category | flops | bytes accessed | tf_op | source)
XLA Modules:
  0.0 59.1 jit_solution(13077277282765986213)
XLA Ops:
  0.0 2.5 %collective-permute-start.1 = (bf16[64,512]{1,0:T(8,128)(2,1)}, bf16[64,512]{1,0:T(8,128)(2,1)S(1)}, u32[]{:S(2)}, u32[]{:S(2)}) collective-permute-start(bf16[64,512]{1,0:T(8,128)(2,1)} %own.1), channel_id=1, source_target_pairs={{0,6},{1,7},{2,0},{3,1},{4,2},{5,3},{6,4},{7,5},{8,14},{9,15},{10,... | collective-permute-start | bytes 196616 | tf_op jit(solution)/shard_map/ppermute | solution.py:36
  2.5 0.0 collective-permute-start
  2.5 1.7 %collective-permute-start.2 = (bf16[64,512]{1,0:T(8,128)(2,1)}, bf16[64,512]{1,0:T(8,128)(2,1)S(1)}, u32[]{:S(2)}, u32[]{:S(2)}) collective-permute-start(bf16[64,512]{1,0:T(8,128)(2,1)} %own.1), channel_id=1, source_target_pairs={{0,4},{1,5},{2,6},{3,7},{4,0},{5,1},{6,2},{7,3},{8,12},{9,13},{10,... | collective-permute-start | bytes 196616 | tf_op jit(solution)/shard_map/ppermute | solution.py:36
  4.2 0.0 collective-permute-done.1.right
  4.2 3.4 %collective-permute-done.left = bf16[64,512]{1,0:T(8,128)(2,1)S(1)} collective-permute-done((bf16[64,512]{1,0:T(8,128)(2,1)}, bf16[64,512]{1,0:T(8,128)(2,1)S(1)}, u32[]{:S(2)}, u32[]{:S(2)}) %collective-permute-start) | collective-permute-done | bytes 65568 | tf_op jit(solution)/shard_map/ppermute | solution.py:36
  7.6 0.3 collective-permute-done.2.far
  7.8 0.0 copy-start
  7.8 0.8 %copy-done = bf16[64,512]{1,0:T(8,128)(2,1)S(1)} copy-done((bf16[64,512]{1,0:T(8,128)(2,1)S(1)}, bf16[64,512]{1,0:T(8,128)(2,1)}, u32[]{:S(2)}) %copy-start) | copy-done | bytes 65560
  8.7 0.5 shard_map.17.window
  9.2 4.1 %collective-permute-start.7 = (bf16[4,64,512]{2,1,0:T(8,128)(2,1)S(1)}, bf16[4,64,512]{2,1,0:T(8,128)(2,1)S(1)}, u32[]{:S(2)}, u32[]{:S(2)}) collective-permute-start(bf16[4,64,512]{2,1,0:T(8,128)(2,1)S(1)} %shard_map.17.window), channel_id=1, source_target_pairs={{0,0},{1,1},{2,160},{3,161},{4,224},{5,225},{6,192},{7,193},{8,200... | collective-permute-start | bytes 786440 | tf_op jit(solution)/shard_map/ppermute | solution.py:36
  13.3 0.5 collective-permute-start.3
  13.8 15.9 %collective-permute-done.7.refs_0_ = bf16[4,64,512]{2,1,0:T(8,128)(2,1)S(1)} collective-permute-done((bf16[4,64,512]{2,1,0:T(8,128)(2,1)S(1)}, bf16[4,64,512]{2,1,0:T(8,128)(2,1)S(1)}, u32[]{:S(2)}, u32[]{:S(2)}) %collective-permute-start.7) | collective-permute-done | bytes 262176 | tf_op jit(solution)/shard_map/ppermute | solution.py:36
  29.7 2.9 %collective-permute-start.8 = (bf16[4,64,512]{2,1,0:T(8,128)(2,1)S(1)}, bf16[4,64,512]{2,1,0:T(8,128)(2,1)S(1)}, u32[]{:S(2)}, u32[]{:S(2)}) collective-permute-start(bf16[4,64,512]{2,1,0:T(8,128)(2,1)S(1)} %collective-permute-done.7.refs_0_), channel_id=1, source_target_pairs={{0,16},{1,17},{2,18},{3,19},{4,20},{5,21},{6,22},{7,23},{8,24},{9,... | collective-permute-start | bytes 786440 | tf_op jit(solution)/shard_map/ppermute | solution.py:36
  32.6 0.0 collective-permute-done.3.refs_0_
  32.6 0.1 collective-permute-start.4
  32.7 3.5 %collective-permute-start.9 = (bf16[4,64,512]{2,1,0:T(8,128)(2,1)S(1)}, bf16[4,64,512]{2,1,0:T(8,128)(2,1)S(1)}, u32[]{:S(2)}, u32[]{:S(2)}) collective-permute-start(bf16[4,64,512]{2,1,0:T(8,128)(2,1)S(1)} %collective-permute-done.7.refs_0_), channel_id=1, source_target_pairs={{0,8},{1,9},{2,10},{3,11},{4,12},{5,13},{6,14},{7,15},{8,0},{9,1},... | collective-permute-start | bytes 786440 | tf_op jit(solution)/shard_map/ppermute | solution.py:36
  36.1 0.3 collective-permute-done.8.refs_1_
  36.4 6.4 %collective-permute-start.10 = (bf16[4,64,512]{2,1,0:T(8,128)(2,1)S(1)}, bf16[4,64,512]{2,1,0:T(8,128)(2,1)S(1)}, u32[]{:S(2)}, u32[]{:S(2)}) collective-permute-start(bf16[4,64,512]{2,1,0:T(8,128)(2,1)S(1)} %collective-permute-done.8.refs_1_), channel_id=1, source_target_pairs={{0,8},{1,9},{2,10},{3,11},{4,12},{5,13},{6,14},{7,15},{8,0},{9,1},... | collective-permute-start | bytes 786440 | tf_op jit(solution)/shard_map/ppermute | solution.py:36
  42.8 1.2 %shard_map.18 = (bf16[4,64,8704]{2,1,0:T(8,128)(2,1)S(1)}, f32[64,128]{1,0:T(8,128)S(1)}) custom-call(bf16[4,64,512]{2,1,0:T(8,128)(2,1)S(1)} %shard_map.17.window), custom_call_target="tpu_custom_call" | custom-call | bytes 17825792 | tf_op jit(solution)/shard_map/pallas_call | solution.py:107
  44.1 0.1 collective-permute-start.5
  44.2 0.0 collective-permute-done.4.refs_1_
  44.2 1.5 %collective-permute-start.6 = (bf16[4,64,512]{2,1,0:T(8,128)(2,1)S(1)}, bf16[4,64,512]{2,1,0:T(8,128)(2,1)S(1)}, u32[]{:S(2)}, u32[]{:S(2)}) collective-permute-start(bf16[4,64,512]{2,1,0:T(8,128)(2,1)S(1)} %collective-permute-done.4.refs_1_), channel_id=1, source_target_pairs={{0,8},{1,9},{2,10},{3,11},{4,12},{5,13},{6,14},{7,15},{8,0},{9,1},... | collective-permute-start | bytes 786440 | tf_op jit(solution)/shard_map/ppermute | solution.py:36
  45.6 0.0 collective-permute-done.9.refs_2_
  45.6 0.0 collective-permute-done.10.refs_3_
  45.7 6.7 %shard_map.19.refs_4_ = bf16[65,64,512]{2,1,0:T(8,128)(2,1)} custom-call(s32[1]{0:T(128)} %bitcast.me, bf16[4,64,8704]{2,1,0:T(8,128)(2,1)S(1)} %get-tuple-element.7.moved, f32[64,128]{1,0:T(8,128)S(1)} %get-tuple-element.8.row_scale, bf16[4,64,512]{2,1,0:T(8,128)(2,1)S(1)} %collective-permute-done.7.refs_0_, ...), custom_call_target="tpu_custom_call" | custom-call | flops 4362076160 | bytes 2129920 | tf_op jit(solution)/shard_map/pallas_call | solution.py:165
  52.3 0.0 collective-permute-done.5.refs_2_
  52.3 0.0 collective-permute-done.6.refs_3_
  52.4 6.7 %shard_map.20 = bf16[65,64,512]{2,1,0:T(8,128)(2,1)} custom-call(s32[1]{0:T(128)} %bitcast.me, bf16[4,64,8704]{2,1,0:T(8,128)(2,1)S(1)} %get-tuple-element.7.moved, f32[64,128]{1,0:T(8,128)S(1)} %get-tuple-element.8.row_scale, bf16[4,64,512]{2,1,0:T(8,128)(2,1)S(1)} %collective-permute-done.3.refs_0_, ...), custom_call_target="tpu_custom_call", output_to_operand_aliasing={{}: (7, {})} | custom-call | flops 4362076160 | bytes 2129920 | tf_op jit(solution)/shard_map/pallas_call | solution.py:165
Async XLA Ops:
  0.0 4.2 %collective-permute-start.1 = (bf16[64,512]{1,0:T(8,128)(2,1)}, bf16[64,512]{1,0:T(8,128)(2,1)S(1)}, u32[]{:S(2)}, u32[]{:S(2)}) collective-permute-start(bf16[64,512]{1,0:T(8,128)(2,1)} %own.1), channel_id=1, source_target_pairs={{0,6},{1,7},{2,0},{3,1},{4,2},{5,3},{6,4},{7,5},{8,14},{9,15},{10,... | collective-permute-start | bytes 196616 | tf_op jit(solution)/shard_map/ppermute | solution.py:36
  2.5 5.1 %collective-permute-start = (bf16[64,512]{1,0:T(8,128)(2,1)}, bf16[64,512]{1,0:T(8,128)(2,1)S(1)}, u32[]{:S(2)}, u32[]{:S(2)}) collective-permute-start(bf16[64,512]{1,0:T(8,128)(2,1)} %own.1), channel_id=1, source_target_pairs={{0,2},{1,3},{2,4},{3,5},{4,6},{5,7},{6,0},{7,1},{8,10},{9,11},{10,... | collective-permute-start | bytes 196616 | tf_op jit(solution)/shard_map/ppermute | solution.py:36
  2.5 5.4 %collective-permute-start.2 = (bf16[64,512]{1,0:T(8,128)(2,1)}, bf16[64,512]{1,0:T(8,128)(2,1)S(1)}, u32[]{:S(2)}, u32[]{:S(2)}) collective-permute-start(bf16[64,512]{1,0:T(8,128)(2,1)} %own.1), channel_id=1, source_target_pairs={{0,4},{1,5},{2,6},{3,7},{4,0},{5,1},{6,2},{7,3},{8,12},{9,13},{10,... | collective-permute-start | bytes 196616 | tf_op jit(solution)/shard_map/ppermute | solution.py:36
  7.8 0.8 %copy-start = (bf16[64,512]{1,0:T(8,128)(2,1)S(1)}, bf16[64,512]{1,0:T(8,128)(2,1)}, u32[]{:S(2)}) copy-start(bf16[64,512]{1,0:T(8,128)(2,1)} %own.1) | copy-start | bytes 196612
  9.2 20.5 %collective-permute-start.7 = (bf16[4,64,512]{2,1,0:T(8,128)(2,1)S(1)}, bf16[4,64,512]{2,1,0:T(8,128)(2,1)S(1)}, u32[]{:S(2)}, u32[]{:S(2)}) collective-permute-start(bf16[4,64,512]{2,1,0:T(8,128)(2,1)S(1)} %shard_map.17.window), channel_id=1, source_target_pairs={{0,0},{1,1},{2,160},{3,161},{4,224},{5,225},{6,192},{7,193},{8,200... | collective-permute-start | bytes 786440 | tf_op jit(solution)/shard_map/ppermute | solution.py:36
  13.3 19.3 %collective-permute-start.3 = (bf16[4,64,512]{2,1,0:T(8,128)(2,1)S(1)}, bf16[4,64,512]{2,1,0:T(8,128)(2,1)S(1)}, u32[]{:S(2)}, u32[]{:S(2)}) collective-permute-start(bf16[4,64,512]{2,1,0:T(8,128)(2,1)S(1)} %shard_map.17.window), channel_id=1, source_target_pairs={{0,64},{1,65},{2,128},{3,129},{4,32},{5,33},{6,96},{7,97},{8,40},{... | collective-permute-start | bytes 786440 | tf_op jit(solution)/shard_map/ppermute | solution.py:36
  29.7 6.7 %collective-permute-start.8 = (bf16[4,64,512]{2,1,0:T(8,128)(2,1)S(1)}, bf16[4,64,512]{2,1,0:T(8,128)(2,1)S(1)}, u32[]{:S(2)}, u32[]{:S(2)}) collective-permute-start(bf16[4,64,512]{2,1,0:T(8,128)(2,1)S(1)} %collective-permute-done.7.refs_0_), channel_id=1, source_target_pairs={{0,16},{1,17},{2,18},{3,19},{4,20},{5,21},{6,22},{7,23},{8,24},{9,... | collective-permute-start | bytes 786440 | tf_op jit(solution)/shard_map/ppermute | solution.py:36
  32.6 11.6 %collective-permute-start.4 = (bf16[4,64,512]{2,1,0:T(8,128)(2,1)S(1)}, bf16[4,64,512]{2,1,0:T(8,128)(2,1)S(1)}, u32[]{:S(2)}, u32[]{:S(2)}) collective-permute-start(bf16[4,64,512]{2,1,0:T(8,128)(2,1)S(1)} %collective-permute-done.3.refs_0_), channel_id=1, source_target_pairs={{0,16},{1,17},{2,18},{3,19},{4,20},{5,21},{6,22},{7,23},{8,24},{9,... | collective-permute-start | bytes 786440 | tf_op jit(solution)/shard_map/ppermute | solution.py:36
  32.7 13.0 %collective-permute-start.9 = (bf16[4,64,512]{2,1,0:T(8,128)(2,1)S(1)}, bf16[4,64,512]{2,1,0:T(8,128)(2,1)S(1)}, u32[]{:S(2)}, u32[]{:S(2)}) collective-permute-start(bf16[4,64,512]{2,1,0:T(8,128)(2,1)S(1)} %collective-permute-done.7.refs_0_), channel_id=1, source_target_pairs={{0,8},{1,9},{2,10},{3,11},{4,12},{5,13},{6,14},{7,15},{8,0},{9,1},... | collective-permute-start | bytes 786440 | tf_op jit(solution)/shard_map/ppermute | solution.py:36
  36.4 9.2 %collective-permute-start.10 = (bf16[4,64,512]{2,1,0:T(8,128)(2,1)S(1)}, bf16[4,64,512]{2,1,0:T(8,128)(2,1)S(1)}, u32[]{:S(2)}, u32[]{:S(2)}) collective-permute-start(bf16[4,64,512]{2,1,0:T(8,128)(2,1)S(1)} %collective-permute-done.8.refs_1_), channel_id=1, source_target_pairs={{0,8},{1,9},{2,10},{3,11},{4,12},{5,13},{6,14},{7,15},{8,0},{9,1},... | collective-permute-start | bytes 786440 | tf_op jit(solution)/shard_map/ppermute | solution.py:36
  44.1 8.3 %collective-permute-start.5 = (bf16[4,64,512]{2,1,0:T(8,128)(2,1)S(1)}, bf16[4,64,512]{2,1,0:T(8,128)(2,1)S(1)}, u32[]{:S(2)}, u32[]{:S(2)}) collective-permute-start(bf16[4,64,512]{2,1,0:T(8,128)(2,1)S(1)} %collective-permute-done.3.refs_0_), channel_id=1, source_target_pairs={{0,8},{1,9},{2,10},{3,11},{4,12},{5,13},{6,14},{7,15},{8,0},{9,1},... | collective-permute-start | bytes 786440 | tf_op jit(solution)/shard_map/ppermute | solution.py:36
  44.2 8.2 %collective-permute-start.6 = (bf16[4,64,512]{2,1,0:T(8,128)(2,1)S(1)}, bf16[4,64,512]{2,1,0:T(8,128)(2,1)S(1)}, u32[]{:S(2)}, u32[]{:S(2)}) collective-permute-start(bf16[4,64,512]{2,1,0:T(8,128)(2,1)S(1)} %collective-permute-done.4.refs_1_), channel_id=1, source_target_pairs={{0,8},{1,9},{2,10},{3,11},{4,12},{5,13},{6,14},{7,15},{8,0},{9,1},... | collective-permute-start | bytes 786440 | tf_op jit(solution)/shard_map/ppermute | solution.py:36

commit v3 on v2

--- a/solution.py
+++ b/solution.py
@@ -19,8 +19,7 @@
 PHASES = 4
 REACH = HALF_LAG // PHASES
 
-DEST = np.array([0, 2, 6, 1, 5, 4, 5, 2, 7, 1, 7, 3, 6, 3, 0, 4, 4, 5, 3, 5, 3, 0, 1, 6, 1, 6, 4, 7, 2, 7, 2, 0, 7, 6, 2, 6, 0, 3, 1, 5, 2, 4, 0, 4, 1, 5, 7, 3, 3, 0, 5, 2, 4, 7, 6, 0, 6, 2, 3, 7, 5, 1, 4, 1, 1, 4, 3, 5, 3, 7, 2, 4, 6, 5, 1, 0, 2, 0, 6, 7, 0, 3, 0, 1, 4, 6, 7, 2, 5, 1, 4, 3, 7, 2, 5, 6, 5, 1, 4, 3, 6, 7, 6, 2, 0, 2, 5, 7, 4, 3, 0, 1, 7, 0, 7, 6, 1, 4, 2, 0, 2, 5, 3, 4, 3, 6, 1, 5]).reshape((4, 2, 4, 2, 2))
-FIRST_BITS = -1900972002
+JUMP = ((2, 0, -2, 4), (-2, 4, 2, 0))
 
 
 def pairs(target):
@@ -48,14 +47,19 @@
     return z, h, 1 - k, x, w
 
 
-def to_columns(o):
-    return lambda z, h, k, x, w: (int(DEST[z // 2, z % 2, x, k, o]), h, k, z // 2, w)
-
-
-def part_of(me, o):
-    bit = lax.rem(me, XS) * ZS + me // (XS * KS * HS)
-    first = lax.shift_right_logical(jnp.int32(FIRST_BITS), bit.astype(jnp.int32)) & 1
-    return first if o == 0 else 1 - first
+def to_columns(z, h, k, x, w):
+    jump = JUMP[k][x]
+    return (z + jump) % ZS, h if jump % 4 == 0 else 1 - h, k, z // 2, w
+
+
+def along_z(step):
+    return lambda z, h, k, x, w: ((z + step) % ZS, h, k, x, w)
+
+
+def held(me, step):
+    h, z = lax.rem(me // (XS * KS), HS), me // (XS * KS * HS)
+    q = (z - 2 * lax.rem(me, XS) + step) & 3
+    return q & 1, h ^ (q >> 1)
 
 
 def window_kernel(me, own, left, right, far, out):
@@ -119,7 +123,7 @@
     )(window)
 
 
-def match_kernel(me, moved, row_scale, *refs):
+def match_kernel(step, me, moved, row_scale, *refs):
     pieces, (out, columns, col_scale) = refs[:4], refs[-3:]
     count, seg = pieces[0].shape[1:]
     samples = seg * XS
@@ -127,7 +131,7 @@
 
     @pl.when(pl.program_id(0) == 0)
     def _():
-        h, k = lax.rem(me[0] // (XS * KS), HS), lax.rem(me[0] // XS, KS)
+        h, k = held(me[0], step)[1], lax.rem(me[0] // XS, KS)
         for piece, at in zip(pieces, (h * 2 + k, 2 - h * 2 + k, h * 2 + 1 - k, 3 - h * 2 - k)):
             row = pl.multiple_of(at * count, count)
             for g in range(XS):
@@ -156,19 +160,19 @@
     out[...] = scaled.astype(jnp.bfloat16)
 
 
-def match(me, o, moved, row_scale, pieces, result, columns):
+def match(me, step, moved, row_scale, pieces, result, columns):
     count, seg = pieces[0].shape[1:]
     samples = seg * XS
     width = 4 * count
     inside = pl.BlockSpec(memory_space=pltpu.VMEM)
     before = [] if result is None else [result]
     return pl.pallas_call(
-        match_kernel,
+        functools.partial(match_kernel, step),
         grid_spec=pltpu.PrefetchScalarGridSpec(
             num_scalar_prefetch=1,
             grid=(LAGS // GROUP,),
             in_specs=[inside] * 6 + [pl.BlockSpec(memory_space=pl.ANY)] * len(before),
-            out_specs=pl.BlockSpec((GROUP, count, width), lambda g, me: (g, 0, part_of(me[0], o))),
+            out_specs=pl.BlockSpec((GROUP, count, width), lambda g, me: (g, 0, held(me[0], step)[0])),
             scratch_shapes=[
                 pltpu.VMEM((XS, width, seg), jnp.bfloat16),
                 pltpu.VMEM((8, width), jnp.float32),
@@ -193,14 +197,15 @@
     far = send(series, along_x(2))
     window = whole_window(me, series, left, right, far)
     moved, row_scale = shifts(window)
-    halves = []
-    for o in range(2):
-        mine = send(window, to_columns(o))
-        beside = send(mine, other_y)
-        halves.append((mine, beside, send(mine, other_core), send(beside, other_core)))
+    mine = send(window, to_columns)
+    mine, moved, row_scale = lax.optimization_barrier((mine, moved, row_scale))
+    beside = send(mine, other_y)
+    above = send(mine, along_z(-1))
+    below = send(mine, along_z(1))
     result = None
-    for o, pieces in enumerate(halves):
-        result = match(me, o, moved, row_scale, pieces, result, 8 * count)
+    for step, (first, second) in enumerate(((mine, beside), (above, below))):
+        pieces = (first, second, send(first, other_core), send(second, other_core))
+        result = match(me, step, moved, row_scale, pieces, result, 8 * count)
     return result
 
 

time: 59.2 us -> 54.4 us (0.919)
  the two profiles are of different devices: /device:TPU:225 before, /device:TPU:1 now
where the time goes in v3:
time: 54.4 us; the launch traced here: 54.3 us
  starting transfers between devices  29.7 us (55%)
  Pallas kernels  15.1 us (28%)
  waiting for transfers between devices  8.52 us (16%)
  local copies, waits for them, and re-layouts  0.84 us (2%)
    ppermute x11, starting transfers between devices, send(): return lax.ppermute(value, AXES, pairs(target))  29.7 us
    pallas_call x2, Pallas kernels, match(): pl.pallas_call(functools.partial(match_kernel, step), grid_spec=pltpu.Pre...  13.4 us
    ppermute x11, waiting for transfers between devices, send(): return lax.ppermute(value, AXES, pairs(target))  8.52 us
    pallas_call x1, Pallas kernels, shifts(): pl.pallas_call(shift_kernel, in_specs=[pl.BlockSpec(memory_space=pltpu.VM...  1.22 us
  transfers between devices with their start and end apart: 11, of which 3 were waited for; matrix products, arithmetic and copies ran while one was open for 0% of the time, Pallas kernels for 15%

profile of v3, /device:TPU:1, one launch (start us, length us, event | category | flops | bytes accessed | tf_op | source)
XLA Modules:
  0.0 54.3 jit_solution(1410088226101209874)
XLA Ops:
  0.0 3.3 %collective-permute-start.1 = (bf16[64,512]{1,0:T(8,128)(2,1)}, bf16[64,512]{1,0:T(8,128)(2,1)S(1)}, u32[]{:S(2)}, u32[]{:S(2)}) collective-permute-start(bf16[64,512]{1,0:T(8,128)(2,1)} %own.1), channel_id=1, source_target_pairs={{0,6},{1,7},{2,0},{3,1},{4,2},{5,3},{6,4},{7,5},{8,14},{9,15},{10,... | collective-permute-start | bytes 196616 | tf_op jit(solution)/shard_map/ppermute | solution.py:35
  3.3 0.0 collective-permute-start
  3.3 1.7 %collective-permute-start.2 = (bf16[64,512]{1,0:T(8,128)(2,1)}, bf16[64,512]{1,0:T(8,128)(2,1)S(1)}, u32[]{:S(2)}, u32[]{:S(2)}) collective-permute-start(bf16[64,512]{1,0:T(8,128)(2,1)} %own.1), channel_id=1, source_target_pairs={{0,4},{1,5},{2,6},{3,7},{4,0},{5,1},{6,2},{7,3},{8,12},{9,13},{10,... | collective-permute-start | bytes 196616 | tf_op jit(solution)/shard_map/ppermute | solution.py:35
  5.0 0.0 collective-permute-done.1.right
  5.0 3.4 %collective-permute-done.left = bf16[64,512]{1,0:T(8,128)(2,1)S(1)} collective-permute-done((bf16[64,512]{1,0:T(8,128)(2,1)}, bf16[64,512]{1,0:T(8,128)(2,1)S(1)}, u32[]{:S(2)}, u32[]{:S(2)}) %collective-permute-start) | collective-permute-done | bytes 65568 | tf_op jit(solution)/shard_map/ppermute | solution.py:35
  8.4 0.3 collective-permute-done.2.far
  8.7 0.0 copy-start
  8.7 0.8 %copy-done = bf16[64,512]{1,0:T(8,128)(2,1)S(1)} copy-done((bf16[64,512]{1,0:T(8,128)(2,1)S(1)}, bf16[64,512]{1,0:T(8,128)(2,1)}, u32[]{:S(2)}) %copy-start) | copy-done | bytes 65560
  9.5 0.5 %shard_map.17.window = bf16[4,64,512]{2,1,0:T(8,128)(2,1)S(1)} custom-call(s32[1]{0:T(128)} %bitcast.me, bf16[64,512]{1,0:T(8,128)(2,1)S(1)} %copy-done, bf16[64,512]{1,0:T(8,128)(2,1)S(1)} %collective-permute-done.left, bf16[64,512]{1,0:T(8,128)(2,1)S(1)} %collective-permute-done.1.right, bf16[64,512]{1,0:T(8,128)(2,1)S(1)} %collective-permute-done.2.far), custom_call_target="tpu_custom_call" | custom-call | tf_op jit(solution)/shard_map/pallas_call | solution.py:78
  10.1 10.6 %collective-permute-start.3 = (bf16[4,64,512]{2,1,0:T(8,128)(2,1)S(1)}, bf16[4,64,512]{2,1,0:T(8,128)(2,1)S(1)}, u32[]{:S(2)}, u32[]{:S(2)}) collective-permute-start(bf16[4,64,512]{2,1,0:T(8,128)(2,1)S(1)} %shard_map.17.window), channel_id=1, source_target_pairs={{0,80},{1,81},{2,0},{3,1},{4,208},{5,209},{6,128},{7,129},{8,216},... | collective-permute-start | bytes 786440 | tf_op jit(solution)/shard_map/ppermute | solution.py:35
  20.6 1.2 %shard_map.18 = (bf16[4,64,8704]{2,1,0:T(8,128)(2,1)S(1)}, f32[64,128]{1,0:T(8,128)S(1)}) custom-call(bf16[4,64,512]{2,1,0:T(8,128)(2,1)S(1)} %shard_map.17.window), custom_call_target="tpu_custom_call" | custom-call | bytes 17825792 | tf_op jit(solution)/shard_map/pallas_call | solution.py:111
  21.9 4.9 %collective-permute-done.3.refs_0_ = bf16[4,64,512]{2,1,0:T(8,128)(2,1)S(1)} collective-permute-done((bf16[4,64,512]{2,1,0:T(8,128)(2,1)S(1)}, bf16[4,64,512]{2,1,0:T(8,128)(2,1)S(1)}, u32[]{:S(2)}, u32[]{:S(2)}) %collective-permute-start.3) | collective-permute-done | bytes 262176 | tf_op jit(solution)/shard_map/ppermute | solution.py:35
  26.7 0.1 collective-permute-start.8
  26.8 0.0 collective-permute-start.5
  26.8 4.2 %collective-permute-start.4 = (bf16[4,64,512]{2,1,0:T(8,128)(2,1)S(1)}, bf16[4,64,512]{2,1,0:T(8,128)(2,1)S(1)}, u32[]{:S(2)}, u32[]{:S(2)}) collective-permute-start(bf16[4,64,512]{2,1,0:T(8,128)(2,1)S(1)} %collective-permute-done.3.refs_0_), channel_id=1, source_target_pairs={{0,224},{1,225},{2,226},{3,227},{4,228},{5,229},{6,230},{7,231},{8... | collective-permute-start | bytes 786440 | tf_op jit(solution)/shard_map/ppermute | solution.py:35
  31.0 5.5 %collective-permute-start.9 = (bf16[4,64,512]{2,1,0:T(8,128)(2,1)S(1)}, bf16[4,64,512]{2,1,0:T(8,128)(2,1)S(1)}, u32[]{:S(2)}, u32[]{:S(2)}) collective-permute-start(bf16[4,64,512]{2,1,0:T(8,128)(2,1)S(1)} %collective-permute-done.3.refs_0_), channel_id=1, source_target_pairs={{0,8},{1,9},{2,10},{3,11},{4,12},{5,13},{6,14},{7,15},{8,0},{9,1},... | collective-permute-start | bytes 786440 | tf_op jit(solution)/shard_map/ppermute | solution.py:35
  36.5 0.0 collective-permute-done.8.refs_1_
  36.5 0.0 collective-permute-start.10
  36.5 0.0 collective-permute-done.5.refs_1_
  36.5 4.3 %collective-permute-start.7 = (bf16[4,64,512]{2,1,0:T(8,128)(2,1)S(1)}, bf16[4,64,512]{2,1,0:T(8,128)(2,1)S(1)}, u32[]{:S(2)}, u32[]{:S(2)}) collective-permute-start(bf16[4,64,512]{2,1,0:T(8,128)(2,1)S(1)} %collective-permute-done.5.refs_1_), channel_id=1, source_target_pairs={{0,8},{1,9},{2,10},{3,11},{4,12},{5,13},{6,14},{7,15},{8,0},{9,1},... | collective-permute-start | bytes 786440 | tf_op jit(solution)/shard_map/ppermute | solution.py:35
  40.9 0.0 collective-permute-done.4.refs_0_
  40.9 0.0 collective-permute-start.6
  40.9 0.0 collective-permute-done.9.refs_2_
  40.9 0.0 collective-permute-done.10.refs_3_
  40.9 6.7 %shard_map.19.refs_4_ = bf16[65,64,512]{2,1,0:T(8,128)(2,1)} custom-call(s32[1]{0:T(128)} %bitcast.me, bf16[4,64,8704]{2,1,0:T(8,128)(2,1)S(1)} %get-tuple-element.12.moved, f32[64,128]{1,0:T(8,128)S(1)} %get-tuple-element.13.row_scale, bf16[4,64,512]{2,1,0:T(8,128)(2,1)S(1)} %collective-permute-done.3.refs_0_, ...), custom_call_target="tpu_custom_call" | custom-call | flops 4362076160 | bytes 2129920 | tf_op jit(solution)/shard_map/pallas_call | solution.py:169
  47.6 0.0 collective-permute-done.7.refs_3_
  47.6 0.0 collective-permute-done.6.refs_2_
  47.6 6.7 %shard_map.20 = bf16[65,64,512]{2,1,0:T(8,128)(2,1)} custom-call(s32[1]{0:T(128)} %bitcast.me, bf16[4,64,8704]{2,1,0:T(8,128)(2,1)S(1)} %get-tuple-element.12.moved, f32[64,128]{1,0:T(8,128)S(1)} %get-tuple-element.13.row_scale, bf16[4,64,512]{2,1,0:T(8,128)(2,1)S(1)} %collective-permute-done.4.refs_0_, ...), custom_call_target="tpu_custom_call", output_to_operand_aliasing={{}: (7, {})} | custom-call | flops 4362076160 | bytes 2129920 | tf_op jit(solution)/shard_map/pallas_call | solution.py:169
Async XLA Ops:
  0.0 5.0 %collective-permute-start.1 = (bf16[64,512]{1,0:T(8,128)(2,1)}, bf16[64,512]{1,0:T(8,128)(2,1)S(1)}, u32[]{:S(2)}, u32[]{:S(2)}) collective-permute-start(bf16[64,512]{1,0:T(8,128)(2,1)} %own.1), channel_id=1, source_target_pairs={{0,6},{1,7},{2,0},{3,1},{4,2},{5,3},{6,4},{7,5},{8,14},{9,15},{10,... | collective-permute-start | bytes 196616 | tf_op jit(solution)/shard_map/ppermute | solution.py:35
  3.3 5.1 %collective-permute-start = (bf16[64,512]{1,0:T(8,128)(2,1)}, bf16[64,512]{1,0:T(8,128)(2,1)S(1)}, u32[]{:S(2)}, u32[]{:S(2)}) collective-permute-start(bf16[64,512]{1,0:T(8,128)(2,1)} %own.1), channel_id=1, source_target_pairs={{0,2},{1,3},{2,4},{3,5},{4,6},{5,7},{6,0},{7,1},{8,10},{9,11},{10,... | collective-permute-start | bytes 196616 | tf_op jit(solution)/shard_map/ppermute | solution.py:35
  3.3 5.4 %collective-permute-start.2 = (bf16[64,512]{1,0:T(8,128)(2,1)}, bf16[64,512]{1,0:T(8,128)(2,1)S(1)}, u32[]{:S(2)}, u32[]{:S(2)}) collective-permute-start(bf16[64,512]{1,0:T(8,128)(2,1)} %own.1), channel_id=1, source_target_pairs={{0,4},{1,5},{2,6},{3,7},{4,0},{5,1},{6,2},{7,3},{8,12},{9,13},{10,... | collective-permute-start | bytes 196616 | tf_op jit(solution)/shard_map/ppermute | solution.py:35
  8.7 0.8 %copy-start = (bf16[64,512]{1,0:T(8,128)(2,1)S(1)}, bf16[64,512]{1,0:T(8,128)(2,1)}, u32[]{:S(2)}) copy-start(bf16[64,512]{1,0:T(8,128)(2,1)} %own.1) | copy-start | bytes 196612
  10.1 16.7 %collective-permute-start.3 = (bf16[4,64,512]{2,1,0:T(8,128)(2,1)S(1)}, bf16[4,64,512]{2,1,0:T(8,128)(2,1)S(1)}, u32[]{:S(2)}, u32[]{:S(2)}) collective-permute-start(bf16[4,64,512]{2,1,0:T(8,128)(2,1)S(1)} %shard_map.17.window), channel_id=1, source_target_pairs={{0,80},{1,81},{2,0},{3,1},{4,208},{5,209},{6,128},{7,129},{8,216},... | collective-permute-start | bytes 786440 | tf_op jit(solution)/shard_map/ppermute | solution.py:35
  26.7 9.8 %collective-permute-start.8 = (bf16[4,64,512]{2,1,0:T(8,128)(2,1)S(1)}, bf16[4,64,512]{2,1,0:T(8,128)(2,1)S(1)}, u32[]{:S(2)}, u32[]{:S(2)}) collective-permute-start(bf16[4,64,512]{2,1,0:T(8,128)(2,1)S(1)} %collective-permute-done.3.refs_0_), channel_id=1, source_target_pairs={{0,16},{1,17},{2,18},{3,19},{4,20},{5,21},{6,22},{7,23},{8,24},{9,... | collective-permute-start | bytes 786440 | tf_op jit(solution)/shard_map/ppermute | solution.py:35
  26.8 9.8 %collective-permute-start.5 = (bf16[4,64,512]{2,1,0:T(8,128)(2,1)S(1)}, bf16[4,64,512]{2,1,0:T(8,128)(2,1)S(1)}, u32[]{:S(2)}, u32[]{:S(2)}) collective-permute-start(bf16[4,64,512]{2,1,0:T(8,128)(2,1)S(1)} %collective-permute-done.3.refs_0_), channel_id=1, source_target_pairs={{0,32},{1,33},{2,34},{3,35},{4,36},{5,37},{6,38},{7,39},{8,40},{9,... | collective-permute-start | bytes 786440 | tf_op jit(solution)/shard_map/ppermute | solution.py:35
  26.8 14.1 %collective-permute-start.4 = (bf16[4,64,512]{2,1,0:T(8,128)(2,1)S(1)}, bf16[4,64,512]{2,1,0:T(8,128)(2,1)S(1)}, u32[]{:S(2)}, u32[]{:S(2)}) collective-permute-start(bf16[4,64,512]{2,1,0:T(8,128)(2,1)S(1)} %collective-permute-done.3.refs_0_), channel_id=1, source_target_pairs={{0,224},{1,225},{2,226},{3,227},{4,228},{5,229},{6,230},{7,231},{8... | collective-permute-start | bytes 786440 | tf_op jit(solution)/shard_map/ppermute | solution.py:35
  31.0 9.9 %collective-permute-start.9 = (bf16[4,64,512]{2,1,0:T(8,128)(2,1)S(1)}, bf16[4,64,512]{2,1,0:T(8,128)(2,1)S(1)}, u32[]{:S(2)}, u32[]{:S(2)}) collective-permute-start(bf16[4,64,512]{2,1,0:T(8,128)(2,1)S(1)} %collective-permute-done.3.refs_0_), channel_id=1, source_target_pairs={{0,8},{1,9},{2,10},{3,11},{4,12},{5,13},{6,14},{7,15},{8,0},{9,1},... | collective-permute-start | bytes 786440 | tf_op jit(solution)/shard_map/ppermute | solution.py:35
  36.5 4.4 %collective-permute-start.10 = (bf16[4,64,512]{2,1,0:T(8,128)(2,1)S(1)}, bf16[4,64,512]{2,1,0:T(8,128)(2,1)S(1)}, u32[]{:S(2)}, u32[]{:S(2)}) collective-permute-start(bf16[4,64,512]{2,1,0:T(8,128)(2,1)S(1)} %collective-permute-done.8.refs_1_), channel_id=1, source_target_pairs={{0,8},{1,9},{2,10},{3,11},{4,12},{5,13},{6,14},{7,15},{8,0},{9,1},... | collective-permute-start | bytes 786440 | tf_op jit(solution)/shard_map/ppermute | solution.py:35
  36.5 11.0 %collective-permute-start.7 = (bf16[4,64,512]{2,1,0:T(8,128)(2,1)S(1)}, bf16[4,64,512]{2,1,0:T(8,128)(2,1)S(1)}, u32[]{:S(2)}, u32[]{:S(2)}) collective-permute-start(bf16[4,64,512]{2,1,0:T(8,128)(2,1)S(1)} %collective-permute-done.5.refs_1_), channel_id=1, source_target_pairs={{0,8},{1,9},{2,10},{3,11},{4,12},{5,13},{6,14},{7,15},{8,0},{9,1},... | collective-permute-start | bytes 786440 | tf_op jit(solution)/shard_map/ppermute | solution.py:35
  40.9 6.7 %collective-permute-start.6 = (bf16[4,64,512]{2,1,0:T(8,128)(2,1)S(1)}, bf16[4,64,512]{2,1,0:T(8,128)(2,1)S(1)}, u32[]{:S(2)}, u32[]{:S(2)}) collective-permute-start(bf16[4,64,512]{2,1,0:T(8,128)(2,1)S(1)} %collective-permute-done.4.refs_0_), channel_id=1, source_target_pairs={{0,8},{1,9},{2,10},{3,11},{4,12},{5,13},{6,14},{7,15},{8,0},{9,1},... | collective-permute-start | bytes 786440 | tf_op jit(solution)/shard_map/ppermute | solution.py:35

commit v4 on v3

v4 whole, which is shorter than its diff:
```python
import functools
import itertools

import jax
import jax.numpy as jnp
import numpy as np
from jax import lax
from jax.experimental import pallas as pl
from jax.experimental.pallas import tpu as pltpu
from jax.sharding import PartitionSpec as P

HALF_LAG = 32
LAGS = 2 * HALF_LAG + 1
AXES = ("chan", "seg", "win")
ZS, HS, KS, XS, WS = 8, 2, 2, 4, 2
EDGE = 128

GROUP = 13
PHASES = 4
REACH = HALF_LAG // PHASES
PAIR = XS // 2
INSIDE = pl.BlockSpec(memory_space=pltpu.VMEM)

JUMP = ((2, 0, -2, 4), (-2, 4, 2, 0))


def pairs(target):
    places = itertools.product(range(ZS), range(HS), range(KS), range(XS), range(WS))
    shape = (ZS, HS, KS, XS, WS)
    return [
        (int(np.ravel_multi_index(p, shape)), int(np.ravel_multi_index(target(*p), shape)))
        for p in places
    ]


def send(value, target):
    return lax.ppermute(value, AXES, pairs(target))


def along_x(step):
    return lambda z, h, k, x, w: (z, h, k, (x + step) % XS, w)


def other_y(z, h, k, x, w):
    return z, 1 - h, k, x, w


def other_core(z, h, k, x, w):
    return z, h, 1 - k, x, w


def to_columns(z, h, k, x, w):
    jump = JUMP[k][x]
    return (z + jump) % ZS, h if jump % 4 == 0 else 1 - h, k, z // 2, w


def along_z(step):
    return lambda z, h, k, x, w: ((z + step) % ZS, h, k, x, w)


def held(me, step):
    h, z = lax.rem(me // (XS * KS), HS), me // (XS * KS * HS)
    q = (z - 2 * lax.rem(me, XS) + step) & 3
    return q & 1, h ^ (q >> 1)


def window_kernel(me, own, left, right, far, early, late):
    x = lax.rem(me[0], XS)
    seg = own.shape[1]
    sample = lax.broadcasted_iota(jnp.int32, (seg, seg), 0)
    place = lax.broadcasted_iota(jnp.int32, (seg, seg), 1)
    move = lax.rem(sample, PHASES) * EDGE + sample // PHASES == place
    move = jnp.where(move, 1.0, 0.0).astype(jnp.bfloat16)
    for piece, step in ((own, 0), (left, XS - 1), (right, 1), (far, 2)):
        values = jnp.dot(piece[...], move, preferred_element_type=jnp.float32)
        values = values.astype(jnp.bfloat16)[None]
        g = lax.rem(x + step, XS)

        @pl.when(g < PAIR)
        def _():
            early[pl.ds(g, 1)] = values

        @pl.when(g >= PAIR)
        def _():
            late[pl.ds(g - PAIR, 1)] = values


def whole_window(me, own, left, right, far):
    return pl.pallas_call(
        window_kernel,
        in_specs=[pl.BlockSpec(memory_space=pltpu.SMEM)] + [INSIDE] * 4,
        out_specs=[INSIDE] * 2,
        out_shape=[jax.ShapeDtypeStruct((PAIR,) + own.shape, own.dtype)] * 2,
        compiler_params=pltpu.CompilerParams(vmem_limit_bytes=16 * 2**20),
    )(me, own, left, right, far)


def shift_kernel(early, late, out, scale):
    count, seg = early.shape[1:]
    window = [early.at[0], early.at[1], late.at[0], late.at[1]]
    edge = jnp.zeros((count, EDGE), jnp.bfloat16)
    total = jnp.zeros((count, 1), jnp.float32)
    for g in range(XS):
        wide = window[g][...].astype(jnp.float32)
        total += jnp.sum(wide * wide, axis=1, keepdims=True)
    samples = seg * XS
    norm = lax.rsqrt(total / samples + 1e-06) * (1.0 / np.sqrt(samples))
    scale[...] = jnp.broadcast_to(norm, scale.shape)
    for j in range(PHASES):
        tiles = [window[g][:, j * EDGE : (j + 1) * EDGE] for g in range(XS)]
        row = jnp.concatenate([edge] + tiles + [edge], axis=1)
        for o in range(2 * REACH + 1):
            moved = pltpu.roll(row, (REACH - o) % row.shape[1], 1)
            at = (PHASES * o + j) * EDGE
            for g in range(XS):
                out[g, :, at : at + EDGE] = moved[:, (g + 1) * EDGE : (g + 2) * EDGE]


def shifts(early, late):
    count, seg = early.shape[1:]
    width = (2 * REACH + 1) * PHASES * EDGE
    return pl.pallas_call(
        shift_kernel,
        in_specs=[INSIDE] * 2,
        out_specs=[INSIDE] * 2,
        out_shape=[
            jax.ShapeDtypeStruct((XS, count, width), jnp.bfloat16),
            jax.ShapeDtypeStruct((count, EDGE), jnp.float32),
        ],
        compiler_params=pltpu.CompilerParams(vmem_limit_bytes=16 * 2**20),
        cost_estimate=pl.CostEstimate(
            flops=0, bytes_accessed=8 * XS * count * width, transcendentals=0
        ),
    )(early, late)


def place_columns(me, pieces, columns):
    count, seg = pieces[0].shape[1:]
    k = lax.rem(me // XS, KS)
    r, h = held(me, 0)
    r_up, h_up = held(me, 1)
    blocks = (r * 2 + h, r * 2 + 1 - h, r_up * 2 + h_up, r_up * 2 + 1 - h_up)
    for n, piece in enumerate(pieces):
        core = k if n < 4 else 1 - k
        row = pl.multiple_of((blocks[n % 4] * 2 + core) * count, count)
        for g in range(PAIR):
            columns[pl.ds(row, count), g * seg : (g + 1) * seg] = piece[g]
    wide = columns[...].astype(jnp.float32)
    total = jnp.sum(wide * wide, axis=1, keepdims=True)
    return jnp.broadcast_to(total, (columns.shape[0], EDGE)).T[:8]


def group_products(moved, columns, first_seg, group):
    seg = columns.shape[1] // PAIR
    last = 2 * HALF_LAG - group * GROUP
    rows = [
        [
            moved[first_seg + g, :, pl.ds(pl.multiple_of((last - u) * EDGE, EDGE), seg)]
            for g in range(PAIR)
        ]
        for u in range(GROUP)
    ]
    rows = jnp.concatenate([jnp.concatenate(row, axis=1) for row in rows], axis=0)
    products = lax.dot_general(
        rows, columns[...], (((1,), (1,)), ((), ())), preferred_element_type=jnp.float32
    )
    return products.reshape(GROUP, rows.shape[0] // GROUP, columns.shape[0])


def early_kernel(me, moved, *refs):
    pieces, (out, energy, columns) = refs[:8], refs[8:]
    energy[...] = place_columns(me[0], pieces, columns)
    for group in range(LAGS // GROUP):
        out[group * GROUP : (group + 1) * GROUP] = group_products(moved, columns, 0, group)


def match_early(me, moved, pieces):
    count, seg = pieces[0].shape[1:]
    width = 8 * count
    return pl.pallas_call(
        early_kernel,
        in_specs=[pl.BlockSpec(memory_space=pltpu.SMEM)] + [INSIDE] * 9,
        out_specs=[INSIDE] * 2,
        out_shape=[
            jax.ShapeDtypeStruct((LAGS, count, width), jnp.float32),
            jax.ShapeDtypeStruct((8, width), jnp.float32),
        ],
        scratch_shapes=[pltpu.VMEM((width, PAIR * seg), jnp.bfloat16)],
        compiler_params=pltpu.CompilerParams(vmem_limit_bytes=32 * 2**20),
        cost_estimate=pl.CostEstimate(
            flops=2 * LAGS * count * width * PAIR * seg, bytes_accessed=0, transcendentals=0
        ),
    )(me, moved, *pieces)


def late_kernel(me, moved, row_scale, before, energy, *refs):
    pieces, (out, columns, col_scale) = refs[:8], refs[8:]
    group = pl.program_id(0)

    @pl.when(group == 0)
    def _():
        total = energy[...] + place_columns(me[0], pieces, columns)
        col_scale[...] = lax.rsqrt(total / (PAIR * columns.shape[1]) + 1e-06)

    products = group_products(moved, columns, PAIR, group)
    products += before[pl.ds(group * GROUP, GROUP)]
    scaled = products * row_scale[:, :1][None] * col_scale[:1][None]
    out[...] = scaled.astype(jnp.bfloat16)


def match_late(me, moved, row_scale, before, energy, pieces):
    count, seg = pieces[0].shape[1:]
    width = 8 * count
    return pl.pallas_call(
        late_kernel,
        grid=(LAGS // GROUP,),
        in_specs=[pl.BlockSpec(memory_space=pltpu.SMEM)] + [INSIDE] * 12,
        out_specs=pl.BlockSpec((GROUP, count, width), lambda g: (g, 0, 0)),
        out_shape=jax.ShapeDtypeStruct((LAGS, count, width), jnp.bfloat16),
        scratch_shapes=[
            pltpu.VMEM((width, PAIR * seg), jnp.bfloat16),
            pltpu.VMEM((8, width), jnp.float32),
        ],
        compiler_params=pltpu.CompilerParams(vmem_limit_bytes=32 * 2**20),
        cost_estimate=pl.CostEstimate(
            flops=2 * LAGS * count * width * PAIR * seg,
            bytes_accessed=2 * LAGS * count * width,
            transcendentals=0,
        ),
    )(me, moved, row_scale, before, energy, *pieces)


def spread(mine):
    return [mine, send(mine, other_y), send(mine, along_z(-1)), send(mine, along_z(1))]


def swap(pieces):
    return [send(piece, other_core) for piece in pieces]


def on_device(series):
    me = (lax.axis_index("chan") * XS + lax.axis_index("seg")).reshape(1)
    left = send(series, along_x(1))
    right = send(series, along_x(-1))
    far = send(series, along_x(2))
    early, late = whole_window(me, series, left, right, far)
    moved, row_scale = shifts(early, late)
    early = send(early, to_columns)
    late = send(late, to_columns)
    early, moved, row_scale = lax.optimization_barrier((early, moved, row_scale))
    early = spread(early)
    late = spread(late)
    partial, energy = match_early(me, moved, early + swap(early))
    *late, partial, energy = lax.optimization_barrier((*late, partial, energy))
    return match_late(me, moved, row_scale, partial, energy, late + swap(late))


def solution(mesh):
    placed = (P("chan", ("win", "seg")),)
    return jax.shard_map(
        on_device, mesh=mesh, in_specs=placed, out_specs=P("win", "chan", "seg"), check_vma=False
    )
```

time: 54.4 us -> 67.7 us (1.24)
  starting transfers between devices: 29.7 us -> 45.8 us
  waiting for transfers between devices: 8.52 us -> 7.07 us
  Pallas kernels: 15.1 us -> 13.8 us
    ppermute x11 -> x19, starting transfers between devices: 29.7 us -> 45.8 us  [send(): return lax.ppermute(value, AXES, pairs(target))]
    pallas_call x3, Pallas kernels: 14.6 us -> 12.8 us  [the longest x1 6.88 us: match_late(): pl.pallas_call(late_kernel, grid=(LAGS // GROUP,), in_specs=[pl.BlockSpec...]
    ppermute x11 -> x19, waiting for transfers between devices: 8.52 us -> 7.07 us  [send(): return lax.ppermute(value, AXES, pairs(target))]
  transfers between devices with their start and end apart: 11 -> 19, of which waited for: 3 -> 7; matrix products, arithmetic and copies ran while one was open for 0% -> 0% of each run, Pallas kernels for 15% -> 9%
where the time goes in v4:
time: 67.7 us; the launch traced here: 67.6 us
  starting transfers between devices  45.8 us (68%)
  Pallas kernels  13.8 us (20%)
  waiting for transfers between devices  7.07 us (10%)
  local copies, waits for them, and re-layouts  0.84 us (1%)
    ppermute x19, starting transfers between devices, send(): return lax.ppermute(value, AXES, pairs(target))  45.8 us
    ppermute x19, waiting for transfers between devices, send(): return lax.ppermute(value, AXES, pairs(target))  7.07 us
    pallas_call x1, Pallas kernels, match_late(): pl.pallas_call(late_kernel, grid=(LAGS // GROUP,), in_specs=[pl.BlockSpec...  6.88 us
    pallas_call x1, Pallas kernels, match_early(): pl.pallas_call(early_kernel, in_specs=[pl.BlockSpec(memory_space=pltpu.SM...  4.75 us
  transfers between devices with their start and end apart: 19, of which 7 were waited for; matrix products, arithmetic and copies ran while one was open for 0% of the time, Pallas kernels for 9%

profile of v4, /device:TPU:1, one launch (start us, length us, event | category | flops | bytes accessed | tf_op | source)
XLA Modules:
  0.0 67.6 jit_solution(2948763157904982130)
XLA Ops:
  0.0 3.3 %collective-permute-start.1 = (bf16[64,512]{1,0:T(8,128)(2,1)}, bf16[64,512]{1,0:T(8,128)(2,1)S(1)}, u32[]{:S(2)}, u32[]{:S(2)}) collective-permute-start(bf16[64,512]{1,0:T(8,128)(2,1)} %own.1), channel_id=1, source_target_pairs={{0,6},{1,7},{2,0},{3,1},{4,2},{5,3},{6,4},{7,5},{8,14},{9,15},{10,... | collective-permute-start | bytes 196616 | tf_op jit(solution)/shard_map/ppermute | solution.py:37
  3.3 1.7 %collective-permute-start.2 = (bf16[64,512]{1,0:T(8,128)(2,1)}, bf16[64,512]{1,0:T(8,128)(2,1)S(1)}, u32[]{:S(2)}, u32[]{:S(2)}) collective-permute-start(bf16[64,512]{1,0:T(8,128)(2,1)} %own.1), channel_id=1, source_target_pairs={{0,4},{1,5},{2,6},{3,7},{4,0},{5,1},{6,2},{7,3},{8,12},{9,13},{10,... | collective-permute-start | bytes 196616 | tf_op jit(solution)/shard_map/ppermute | solution.py:37
  5.0 0.0 collective-permute-done.1.right
  5.0 3.4 %collective-permute-done.left = bf16[64,512]{1,0:T(8,128)(2,1)S(1)} collective-permute-done((bf16[64,512]{1,0:T(8,128)(2,1)}, bf16[64,512]{1,0:T(8,128)(2,1)S(1)}, u32[]{:S(2)}, u32[]{:S(2)}) %collective-permute-start) | collective-permute-done | bytes 65568 | tf_op jit(solution)/shard_map/ppermute | solution.py:37
  8.4 0.3 collective-permute-done.2.far
  8.7 0.8 %copy-done = bf16[64,512]{1,0:T(8,128)(2,1)S(1)} copy-done((bf16[64,512]{1,0:T(8,128)(2,1)S(1)}, bf16[64,512]{1,0:T(8,128)(2,1)}, u32[]{:S(2)}) %copy-start) | copy-done | bytes 65560
  9.5 0.9 %shard_map.17 = (bf16[2,64,512]{2,1,0:T(8,128)(2,1)S(1)}, bf16[2,64,512]{2,1,0:T(8,128)(2,1)S(1)}) custom-call(s32[1]{0:T(128)} %bitcast.me, bf16[64,512]{1,0:T(8,128)(2,1)S(1)} %copy-done, bf16[64,512]{1,0:T(8,128)(2,1)S(1)} %collective-permute-done.left, bf16[64,512]{1,0:T(8,128)(2,1)S(1)} %collective-permute-done.1.right, ...), custom_call_target="tpu_custom_call" | custom-call | tf_op jit(solution)/shard_map/pallas_call | solution.py:89
  10.4 10.6 %collective-permute-start.3 = (bf16[2,64,512]{2,1,0:T(8,128)(2,1)S(1)}, bf16[2,64,512]{2,1,0:T(8,128)(2,1)S(1)}, u32[]{:S(2)}, u32[]{:S(2)}) collective-permute-start(bf16[2,64,512]{2,1,0:T(8,128)(2,1)S(1)} %get-tuple-element.20.early), channel_id=1, source_target_pairs={{0,80},{1,81},{2,0},{3,1},{4,208},{5,209},{6,128},{7,129},{8,216},... | collective-permute-start | bytes 393224 | tf_op jit(solution)/shard_map/ppermute | solution.py:37
  21.0 1.2 %shard_map.18 = (bf16[4,64,8704]{2,1,0:T(8,128)(2,1)S(1)}, f32[64,128]{1,0:T(8,128)S(1)}) custom-call(bf16[2,64,512]{2,1,0:T(8,128)(2,1)S(1)} %get-tuple-element.20.early, bf16[2,64,512]{2,1,0:T(8,128)(2,1)S(1)} %get-tuple-element.21.late), custom_call_target="tpu_custom_call" | custom-call | bytes 17825792 | tf_op jit(solution)/shard_map/pallas_call | solution.py:122
  22.2 2.1 %collective-permute-done.3.refs_0_ = bf16[2,64,512]{2,1,0:T(8,128)(2,1)S(1)} collective-permute-done((bf16[2,64,512]{2,1,0:T(8,128)(2,1)S(1)}, bf16[2,64,512]{2,1,0:T(8,128)(2,1)S(1)}, u32[]{:S(2)}, u32[]{:S(2)}) %collective-permute-start.3) | collective-permute-done | bytes 131104 | tf_op jit(solution)/shard_map/ppermute | solution.py:37
  24.3 2.7 %collective-permute-start.9 = (bf16[2,64,512]{2,1,0:T(8,128)(2,1)S(1)}, bf16[2,64,512]{2,1,0:T(8,128)(2,1)S(1)}, u32[]{:S(2)}, u32[]{:S(2)}) collective-permute-start(bf16[2,64,512]{2,1,0:T(8,128)(2,1)S(1)} %collective-permute-done.3.refs_0_), channel_id=1, source_target_pairs={{0,224},{1,225},{2,226},{3,227},{4,228},{5,229},{6,230},{7,231},{8... | collective-permute-start | bytes 393224 | tf_op jit(solution)/shard_map/ppermute | solution.py:37
  27.0 2.3 %collective-permute-start.8 = (bf16[2,64,512]{2,1,0:T(8,128)(2,1)S(1)}, bf16[2,64,512]{2,1,0:T(8,128)(2,1)S(1)}, u32[]{:S(2)}, u32[]{:S(2)}) collective-permute-start(bf16[2,64,512]{2,1,0:T(8,128)(2,1)S(1)} %collective-permute-done.3.refs_0_), channel_id=1, source_target_pairs={{0,16},{1,17},{2,18},{3,19},{4,20},{5,21},{6,22},{7,23},{8,24},{9,... | collective-permute-start | bytes 393224 | tf_op jit(solution)/shard_map/ppermute | solution.py:37
  29.2 4.9 %collective-permute-start.4 = (bf16[2,64,512]{2,1,0:T(8,128)(2,1)S(1)}, bf16[2,64,512]{2,1,0:T(8,128)(2,1)S(1)}, u32[]{:S(2)}, u32[]{:S(2)}) collective-permute-start(bf16[2,64,512]{2,1,0:T(8,128)(2,1)S(1)} %get-tuple-element.21.late), channel_id=1, source_target_pairs={{0,80},{1,81},{2,0},{3,1},{4,208},{5,209},{6,128},{7,129},{8,216},... | collective-permute-start | bytes 393224 | tf_op jit(solution)/shard_map/ppermute | solution.py:37
  34.2 3.3 %collective-permute-start.11 = (bf16[2,64,512]{2,1,0:T(8,128)(2,1)S(1)}, bf16[2,64,512]{2,1,0:T(8,128)(2,1)S(1)}, u32[]{:S(2)}, u32[]{:S(2)}) collective-permute-start(bf16[2,64,512]{2,1,0:T(8,128)(2,1)S(1)} %collective-permute-done.3.refs_0_), channel_id=1, source_target_pairs={{0,8},{1,9},{2,10},{3,11},{4,12},{5,13},{6,14},{7,15},{8,0},{9,1},... | collective-permute-start | bytes 393224 | tf_op jit(solution)/shard_map/ppermute | solution.py:37
  37.5 0.0 collective-permute-done.10.refs_3_
  37.5 0.1 collective-permute-start.14
  37.6 0.4 collective-permute-start.13
  38.0 0.0 collective-permute-done.8.refs_1_
  38.0 0.7 %collective-permute-start.12 = (bf16[2,64,512]{2,1,0:T(8,128)(2,1)S(1)}, bf16[2,64,512]{2,1,0:T(8,128)(2,1)S(1)}, u32[]{:S(2)}, u32[]{:S(2)}) collective-permute-start(bf16[2,64,512]{2,1,0:T(8,128)(2,1)S(1)} %collective-permute-done.8.refs_1_), channel_id=1, source_target_pairs={{0,8},{1,9},{2,10},{3,11},{4,12},{5,13},{6,14},{7,15},{8,0},{9,1},... | collective-permute-start | bytes 393224 | tf_op jit(solution)/shard_map/ppermute | solution.py:37
  38.7 1.3 %collective-permute-start.7 = (bf16[2,64,512]{2,1,0:T(8,128)(2,1)S(1)}, bf16[2,64,512]{2,1,0:T(8,128)(2,1)S(1)}, u32[]{:S(2)}, u32[]{:S(2)}) collective-permute-start(bf16[2,64,512]{2,1,0:T(8,128)(2,1)S(1)} %collective-permute-done.4.refs_0_), channel_id=1, source_target_pairs={{0,32},{1,33},{2,34},{3,35},{4,36},{5,37},{6,38},{7,39},{8,40},{9,... | collective-permute-start | bytes 393224 | tf_op jit(solution)/shard_map/ppermute | solution.py:37
  40.0 2.6 %collective-permute-start.6 = (bf16[2,64,512]{2,1,0:T(8,128)(2,1)S(1)}, bf16[2,64,512]{2,1,0:T(8,128)(2,1)S(1)}, u32[]{:S(2)}, u32[]{:S(2)}) collective-permute-start(bf16[2,64,512]{2,1,0:T(8,128)(2,1)S(1)} %collective-permute-done.4.refs_0_), channel_id=1, source_target_pairs={{0,224},{1,225},{2,226},{3,227},{4,228},{5,229},{6,230},{7,231},{8... | collective-permute-start | bytes 393224 | tf_op jit(solution)/shard_map/ppermute | solution.py:37
  42.6 1.9 %collective-permute-start.5 = (bf16[2,64,512]{2,1,0:T(8,128)(2,1)S(1)}, bf16[2,64,512]{2,1,0:T(8,128)(2,1)S(1)}, u32[]{:S(2)}, u32[]{:S(2)}) collective-permute-start(bf16[2,64,512]{2,1,0:T(8,128)(2,1)S(1)} %collective-permute-done.4.refs_0_), channel_id=1, source_target_pairs={{0,16},{1,17},{2,18},{3,19},{4,20},{5,21},{6,22},{7,23},{8,24},{9,... | collective-permute-start | bytes 393224 | tf_op jit(solution)/shard_map/ppermute | solution.py:37
  44.5 4.7 %shard_map.19 = (f32[65,64,512]{2,1,0:T(8,128)S(1)}, f32[8,512]{1,0:T(8,128)S(1)}) custom-call(s32[1]{0:T(128)} %bitcast.me, bf16[4,64,8704]{2,1,0:T(8,128)(2,1)S(1)} %get-tuple-element.24.moved, bf16[2,64,512]{2,1,0:T(8,128)(2,1)S(1)} %collective-permute-done.3.refs_0_, bf16[2,64,512]{2,1,0:T(8,128)(2,1)S(1)} %collective-permute-done.8.refs_1_, ...), custom_call_target="tpu_custom_call" | custom-call | flops 4362076160 | tf_op jit(solution)/shard_map/pallas_call | solution.py:180
  49.3 9.6 %collective-permute-start.15 = (bf16[2,64,512]{2,1,0:T(8,128)(2,1)S(1)}, bf16[2,64,512]{2,1,0:T(8,128)(2,1)S(1)}, u32[]{:S(2)}, u32[]{:S(2)}) collective-permute-start(bf16[2,64,512]{2,1,0:T(8,128)(2,1)S(1)} %collective-permute-done.4.refs_0_), channel_id=1, source_target_pairs={{0,8},{1,9},{2,10},{3,11},{4,12},{5,13},{6,14},{7,15},{8,0},{9,1},... | collective-permute-start | bytes 393224 | tf_op jit(solution)/shard_map/ppermute | solution.py:37
  58.8 0.0 collective-permute-start.16
  58.8 0.5 collective-permute-start.17
  59.3 0.0 collective-permute-start.18
  59.3 0.5 collective-permute-done.15.refs_4_
  59.8 0.4 collective-permute-done.16.refs_5_
  60.2 0.2 collective-permute-done.17.refs_6_
  60.4 0.3 collective-permute-done.18.refs_7_
  60.7 6.9 %shard_map.20 = bf16[65,64,512]{2,1,0:T(8,128)(2,1)} custom-call(s32[1]{0:T(128)} %bitcast.me, bf16[4,64,8704]{2,1,0:T(8,128)(2,1)S(1)} %get-tuple-element.24.moved, f32[64,128]{1,0:T(8,128)S(1)} %get-tuple-element.25.row_scale, f32[65,64,512]{2,1,0:T(8,128)S(1)} %get-tuple-element.29.before, f32[8,512]{1,0:T(8,128)S(1)} %get-tuple-element.30.energy, ...), custom_call_target="tpu_custom_call" | custom-call | flops 4362076160 | bytes 4259840 | tf_op jit(solution)/shard_map/pallas_call | solution.py:214
  (12 shorter events, 0.0 us)
Async XLA Ops:
  0.0 5.0 %collective-permute-start.1 = (bf16[64,512]{1,0:T(8,128)(2,1)}, bf16[64,512]{1,0:T(8,128)(2,1)S(1)}, u32[]{:S(2)}, u32[]{:S(2)}) collective-permute-start(bf16[64,512]{1,0:T(8,128)(2,1)} %own.1), channel_id=1, source_target_pairs={{0,6},{1,7},{2,0},{3,1},{4,2},{5,3},{6,4},{7,5},{8,14},{9,15},{10,... | collective-permute-start | bytes 196616 | tf_op jit(solution)/shard_map/ppermute | solution.py:37
  3.3 5.1 %collective-permute-start = (bf16[64,512]{1,0:T(8,128)(2,1)}, bf16[64,512]{1,0:T(8,128)(2,1)S(1)}, u32[]{:S(2)}, u32[]{:S(2)}) collective-permute-start(bf16[64,512]{1,0:T(8,128)(2,1)} %own.1), channel_id=1, source_target_pairs={{0,2},{1,3},{2,4},{3,5},{4,6},{5,7},{6,0},{7,1},{8,10},{9,11},{10,... | collective-permute-start | bytes 196616 | tf_op jit(solution)/shard_map/ppermute | solution.py:37
  3.3 5.4 %collective-permute-start.2 = (bf16[64,512]{1,0:T(8,128)(2,1)}, bf16[64,512]{1,0:T(8,128)(2,1)S(1)}, u32[]{:S(2)}, u32[]{:S(2)}) collective-permute-start(bf16[64,512]{1,0:T(8,128)(2,1)} %own.1), channel_id=1, source_target_pairs={{0,4},{1,5},{2,6},{3,7},{4,0},{5,1},{6,2},{7,3},{8,12},{9,13},{10,... | collective-permute-start | bytes 196616 | tf_op jit(solution)/shard_map/ppermute | solution.py:37
  8.7 0.8 %copy-start = (bf16[64,512]{1,0:T(8,128)(2,1)S(1)}, bf16[64,512]{1,0:T(8,128)(2,1)}, u32[]{:S(2)}) copy-start(bf16[64,512]{1,0:T(8,128)(2,1)} %own.1) | copy-start | bytes 196612
  10.4 13.9 %collective-permute-start.3 = (bf16[2,64,512]{2,1,0:T(8,128)(2,1)S(1)}, bf16[2,64,512]{2,1,0:T(8,128)(2,1)S(1)}, u32[]{:S(2)}, u32[]{:S(2)}) collective-permute-start(bf16[2,64,512]{2,1,0:T(8,128)(2,1)S(1)} %get-tuple-element.20.early), channel_id=1, source_target_pairs={{0,80},{1,81},{2,0},{3,1},{4,208},{5,209},{6,128},{7,129},{8,216},... | collective-permute-start | bytes 393224 | tf_op jit(solution)/shard_map/ppermute | solution.py:37
  24.3 13.2 %collective-permute-start.10 = (bf16[2,64,512]{2,1,0:T(8,128)(2,1)S(1)}, bf16[2,64,512]{2,1,0:T(8,128)(2,1)S(1)}, u32[]{:S(2)}, u32[]{:S(2)}) collective-permute-start(bf16[2,64,512]{2,1,0:T(8,128)(2,1)S(1)} %collective-permute-done.3.refs_0_), channel_id=1, source_target_pairs={{0,32},{1,33},{2,34},{3,35},{4,36},{5,37},{6,38},{7,39},{8,40},{9,... | collective-permute-start | bytes 393224 | tf_op jit(solution)/shard_map/ppermute | solution.py:37
  24.3 13.3 %collective-permute-start.9 = (bf16[2,64,512]{2,1,0:T(8,128)(2,1)S(1)}, bf16[2,64,512]{2,1,0:T(8,128)(2,1)S(1)}, u32[]{:S(2)}, u32[]{:S(2)}) collective-permute-start(bf16[2,64,512]{2,1,0:T(8,128)(2,1)S(1)} %collective-permute-done.3.refs_0_), channel_id=1, source_target_pairs={{0,224},{1,225},{2,226},{3,227},{4,228},{5,229},{6,230},{7,231},{8... | collective-permute-start | bytes 393224 | tf_op jit(solution)/shard_map/ppermute | solution.py:37
  27.0 11.0 %collective-permute-start.8 = (bf16[2,64,512]{2,1,0:T(8,128)(2,1)S(1)}, bf16[2,64,512]{2,1,0:T(8,128)(2,1)S(1)}, u32[]{:S(2)}, u32[]{:S(2)}) collective-permute-start(bf16[2,64,512]{2,1,0:T(8,128)(2,1)S(1)} %collective-permute-done.3.refs_0_), channel_id=1, source_target_pairs={{0,16},{1,17},{2,18},{3,19},{4,20},{5,21},{6,22},{7,23},{8,24},{9,... | collective-permute-start | bytes 393224 | tf_op jit(solution)/shard_map/ppermute | solution.py:37
  29.2 9.4 %collective-permute-start.4 = (bf16[2,64,512]{2,1,0:T(8,128)(2,1)S(1)}, bf16[2,64,512]{2,1,0:T(8,128)(2,1)S(1)}, u32[]{:S(2)}, u32[]{:S(2)}) collective-permute-start(bf16[2,64,512]{2,1,0:T(8,128)(2,1)S(1)} %get-tuple-element.21.late), channel_id=1, source_target_pairs={{0,80},{1,81},{2,0},{3,1},{4,208},{5,209},{6,128},{7,129},{8,216},... | collective-permute-start | bytes 393224 | tf_op jit(solution)/shard_map/ppermute | solution.py:37
  34.2 5.8 %collective-permute-start.11 = (bf16[2,64,512]{2,1,0:T(8,128)(2,1)S(1)}, bf16[2,64,512]{2,1,0:T(8,128)(2,1)S(1)}, u32[]{:S(2)}, u32[]{:S(2)}) collective-permute-start(bf16[2,64,512]{2,1,0:T(8,128)(2,1)S(1)} %collective-permute-done.3.refs_0_), channel_id=1, source_target_pairs={{0,8},{1,9},{2,10},{3,11},{4,12},{5,13},{6,14},{7,15},{8,0},{9,1},... | collective-permute-start | bytes 393224 | tf_op jit(solution)/shard_map/ppermute | solution.py:37
  37.5 5.1 %collective-permute-start.14 = (bf16[2,64,512]{2,1,0:T(8,128)(2,1)S(1)}, bf16[2,64,512]{2,1,0:T(8,128)(2,1)S(1)}, u32[]{:S(2)}, u32[]{:S(2)}) collective-permute-start(bf16[2,64,512]{2,1,0:T(8,128)(2,1)S(1)} %collective-permute-done.10.refs_3_), channel_id=1, source_target_pairs={{0,8},{1,9},{2,10},{3,11},{4,12},{5,13},{6,14},{7,15},{8,0},{9,1},... | collective-permute-start | bytes 393224 | tf_op jit(solution)/shard_map/ppermute | solution.py:37
  37.6 6.9 %collective-permute-start.13 = (bf16[2,64,512]{2,1,0:T(8,128)(2,1)S(1)}, bf16[2,64,512]{2,1,0:T(8,128)(2,1)S(1)}, u32[]{:S(2)}, u32[]{:S(2)}) collective-permute-start(bf16[2,64,512]{2,1,0:T(8,128)(2,1)S(1)} %collective-permute-done.9.refs_2_), channel_id=1, source_target_pairs={{0,8},{1,9},{2,10},{3,11},{4,12},{5,13},{6,14},{7,15},{8,0},{9,1},... | collective-permute-start | bytes 393224 | tf_op jit(solution)/shard_map/ppermute | solution.py:37
  38.0 6.5 %collective-permute-start.12 = (bf16[2,64,512]{2,1,0:T(8,128)(2,1)S(1)}, bf16[2,64,512]{2,1,0:T(8,128)(2,1)S(1)}, u32[]{:S(2)}, u32[]{:S(2)}) collective-permute-start(bf16[2,64,512]{2,1,0:T(8,128)(2,1)S(1)} %collective-permute-done.8.refs_1_), channel_id=1, source_target_pairs={{0,8},{1,9},{2,10},{3,11},{4,12},{5,13},{6,14},{7,15},{8,0},{9,1},... | collective-permute-start | bytes 393224 | tf_op jit(solution)/shard_map/ppermute | solution.py:37
  38.7 10.6 %collective-permute-start.7 = (bf16[2,64,512]{2,1,0:T(8,128)(2,1)S(1)}, bf16[2,64,512]{2,1,0:T(8,128)(2,1)S(1)}, u32[]{:S(2)}, u32[]{:S(2)}) collective-permute-start(bf16[2,64,512]{2,1,0:T(8,128)(2,1)S(1)} %collective-permute-done.4.refs_0_), channel_id=1, source_target_pairs={{0,32},{1,33},{2,34},{3,35},{4,36},{5,37},{6,38},{7,39},{8,40},{9,... | collective-permute-start | bytes 393224 | tf_op jit(solution)/shard_map/ppermute | solution.py:37
  40.0 9.3 %collective-permute-start.6 = (bf16[2,64,512]{2,1,0:T(8,128)(2,1)S(1)}, bf16[2,64,512]{2,1,0:T(8,128)(2,1)S(1)}, u32[]{:S(2)}, u32[]{:S(2)}) collective-permute-start(bf16[2,64,512]{2,1,0:T(8,128)(2,1)S(1)} %collective-permute-done.4.refs_0_), channel_id=1, source_target_pairs={{0,224},{1,225},{2,226},{3,227},{4,228},{5,229},{6,230},{7,231},{8... | collective-permute-start | bytes 393224 | tf_op jit(solution)/shard_map/ppermute | solution.py:37
  42.6 6.7 %collective-permute-start.5 = (bf16[2,64,512]{2,1,0:T(8,128)(2,1)S(1)}, bf16[2,64,512]{2,1,0:T(8,128)(2,1)S(1)}, u32[]{:S(2)}, u32[]{:S(2)}) collective-permute-start(bf16[2,64,512]{2,1,0:T(8,128)(2,1)S(1)} %collective-permute-done.4.refs_0_), channel_id=1, source_target_pairs={{0,16},{1,17},{2,18},{3,19},{4,20},{5,21},{6,22},{7,23},{8,24},{9,... | collective-permute-start | bytes 393224 | tf_op jit(solution)/shard_map/ppermute | solution.py:37
  49.3 10.5 %collective-permute-start.15 = (bf16[2,64,512]{2,1,0:T(8,128)(2,1)S(1)}, bf16[2,64,512]{2,1,0:T(8,128)(2,1)S(1)}, u32[]{:S(2)}, u32[]{:S(2)}) collective-permute-start(bf16[2,64,512]{2,1,0:T(8,128)(2,1)S(1)} %collective-permute-done.4.refs_0_), channel_id=1, source_target_pairs={{0,8},{1,9},{2,10},{3,11},{4,12},{5,13},{6,14},{7,15},{8,0},{9,1},... | collective-permute-start | bytes 393224 | tf_op jit(solution)/shard_map/ppermute | solution.py:37
  58.8 1.3 %collective-permute-start.16 = (bf16[2,64,512]{2,1,0:T(8,128)(2,1)S(1)}, bf16[2,64,512]{2,1,0:T(8,128)(2,1)S(1)}, u32[]{:S(2)}, u32[]{:S(2)}) collective-permute-start(bf16[2,64,512]{2,1,0:T(8,128)(2,1)S(1)} %collective-permute-done.5.refs_1_), channel_id=1, source_target_pairs={{0,8},{1,9},{2,10},{3,11},{4,12},{5,13},{6,14},{7,15},{8,0},{9,1},... | collective-permute-start | bytes 393224 | tf_op jit(solution)/shard_map/ppermute | solution.py:37
  58.8 1.5 %collective-permute-start.17 = (bf16[2,64,512]{2,1,0:T(8,128)(2,1)S(1)}, bf16[2,64,512]{2,1,0:T(8,128)(2,1)S(1)}, u32[]{:S(2)}, u32[]{:S(2)}) collective-permute-start(bf16[2,64,512]{2,1,0:T(8,128)(2,1)S(1)} %collective-permute-done.6.refs_2_), channel_id=1, source_target_pairs={{0,8},{1,9},{2,10},{3,11},{4,12},{5,13},{6,14},{7,15},{8,0},{9,1},... | collective-permute-start | bytes 393224 | tf_op jit(solution)/shard_map/ppermute | solution.py:37
  59.3 1.3 %collective-permute-start.18 = (bf16[2,64,512]{2,1,0:T(8,128)(2,1)S(1)}, bf16[2,64,512]{2,1,0:T(8,128)(2,1)S(1)}, u32[]{:S(2)}, u32[]{:S(2)}) collective-permute-start(bf16[2,64,512]{2,1,0:T(8,128)(2,1)S(1)} %collective-permute-done.7.refs_3_), channel_id=1, source_target_pairs={{0,8},{1,9},{2,10},{3,11},{4,12},{5,13},{6,14},{7,15},{8,0},{9,1},... | collective-permute-start | bytes 393224 | tf_op jit(solution)/shard_map/ppermute | solution.py:37

commit v5 on v3

v5 whole, which is shorter than its diff:
```python
import functools
import itertools

import jax
import jax.numpy as jnp
import numpy as np
from jax import lax
from jax.experimental import pallas as pl
from jax.experimental.pallas import tpu as pltpu
from jax.sharding import PartitionSpec as P

HALF_LAG = 32
LAGS = 2 * HALF_LAG + 1
AXES = ("chan", "seg", "win")
ZS, HS, KS, XS, WS = 8, 2, 2, 4, 2
EDGE = 128

PHASES = 4
REACH = HALF_LAG // PHASES
TILES = 2 * (2 * REACH + 1)
BLOCKS = (range(0, 11), range(11, 22), range(22, HALF_LAG + 1))
INSIDE = pl.BlockSpec(memory_space=pltpu.VMEM)
ANYWHERE = pl.BlockSpec(memory_space=pl.ANY)
SCALAR = pl.BlockSpec(memory_space=pltpu.SMEM)

JUMP = ((2, 0, -2, 4), (-2, 4, 2, 0))


def pairs(target):
    places = itertools.product(range(ZS), range(HS), range(KS), range(XS), range(WS))
    shape = (ZS, HS, KS, XS, WS)
    return [
        (int(np.ravel_multi_index(p, shape)), int(np.ravel_multi_index(target(*p), shape)))
        for p in places
    ]


def send(value, target):
    return lax.ppermute(value, AXES, pairs(target))


def along_x(step):
    return lambda z, h, k, x, w: (z, h, k, (x + step) % XS, w)


def other_y(z, h, k, x, w):
    return z, 1 - h, k, x, w


def other_core(z, h, k, x, w):
    return z, h, 1 - k, x, w


def to_columns(z, h, k, x, w):
    jump = JUMP[k][x]
    return (z + jump) % ZS, h if jump % 4 == 0 else 1 - h, k, z // 2, w


def along_z(step):
    return lambda z, h, k, x, w: ((z + step) % ZS, h, k, x, w)


def held(me, step):
    h, z = lax.rem(me // (XS * KS), HS), me // (XS * KS * HS)
    q = (z - 2 * lax.rem(me, XS) + step) & 3
    return q & 1, h ^ (q >> 1)


def own_kernel(series, out, move, rows, sem):
    copy = pltpu.make_async_copy(series, rows, sem)
    copy.start()
    seg = series.shape[1]
    sample = lax.broadcasted_iota(jnp.int32, (seg, seg), 0)
    place = lax.broadcasted_iota(jnp.int32, (seg, seg), 1)
    goes = (sample & (PHASES - 1)) * EDGE + sample // PHASES == place
    move[...] = jnp.where(goes, 1.0, 0.0).astype(jnp.bfloat16)
    copy.wait()
    values = jnp.dot(rows[...], move[...], preferred_element_type=jnp.float32)
    out[...] = values.astype(jnp.bfloat16)


def own_segment(series):
    count, seg = series.shape
    return pl.pallas_call(
        own_kernel,
        in_specs=[ANYWHERE],
        out_specs=[INSIDE] * 2,
        out_shape=[
            jax.ShapeDtypeStruct((count, seg), jnp.bfloat16),
            jax.ShapeDtypeStruct((seg, seg), jnp.bfloat16),
        ],
        scratch_shapes=[pltpu.VMEM((count, seg), jnp.bfloat16), pltpu.SemaphoreType.DMA],
        compiler_params=pltpu.CompilerParams(vmem_limit_bytes=16 * 2**20),
        cost_estimate=pl.CostEstimate(
            flops=2 * count * seg * seg, bytes_accessed=2 * 2**20, transcendentals=0
        ),
    )(series)


def window_kernel(me, own, move, left, right, far, out):
    x = lax.rem(me[0], XS)
    out[pl.ds(x, 1)] = own[...][None]
    for piece, step in ((left, XS - 1), (right, 1), (far, 2)):
        values = jnp.dot(piece[...], move[...], preferred_element_type=jnp.float32)
        out[pl.ds(lax.rem(x + step, XS), 1)] = values.astype(jnp.bfloat16)[None]


def whole_window(me, own, move, left, right, far):
    return pl.pallas_call(
        window_kernel,
        in_specs=[SCALAR] + [INSIDE] * 5,
        out_specs=INSIDE,
        out_shape=jax.ShapeDtypeStruct((XS,) + own.shape, own.dtype),
        compiler_params=pltpu.CompilerParams(vmem_limit_bytes=16 * 2**20),
    )(me, own, move, left, right, far)


def shift_kernel(window, even, odd, both, scale):
    count, seg = window.shape[1:]
    edge = jnp.zeros((count, EDGE), jnp.bfloat16)
    total = jnp.zeros((count, 1), jnp.float32)
    for g in range(XS):
        wide = window[g].astype(jnp.float32)
        total += jnp.sum(wide * wide, axis=1, keepdims=True)
    samples = seg * XS
    norm = lax.rsqrt(total / samples + 1e-06) * (1.0 / np.sqrt(samples))
    scale[...] = jnp.broadcast_to(norm, scale.shape)
    phase = []
    for j in range(PHASES):
        tiles = [window[g, :, j * EDGE : (j + 1) * EDGE] for g in range(XS)]
        phase.append(jnp.concatenate([edge] + tiles + [edge], axis=1))
    wide = [row.astype(jnp.float32) for row in phase]
    sums = [wide[0] + pltpu.roll(wide[3], 1, 1), wide[2] + wide[1]]
    sums = [row.astype(jnp.bfloat16) for row in sums]
    for out, rows in ((even, phase[0::2]), (odd, phase[1::2]), (both, sums)):
        for a, row in enumerate(rows):
            for o in range(2 * REACH + 1):
                moved = pltpu.roll(row, (REACH - o) % row.shape[1], 1)
                at = (2 * o + a) * EDGE
                for g in range(XS):
                    out[g, :, at : at + EDGE] = moved[:, (g + 1) * EDGE : (g + 2) * EDGE]


def shifts(window):
    count = window.shape[1]
    shape = (XS, count, TILES * EDGE)
    return pl.pallas_call(
        shift_kernel,
        in_specs=[INSIDE],
        out_specs=[INSIDE] * 4,
        out_shape=[jax.ShapeDtypeStruct(shape, jnp.bfloat16)] * 3
        + [jax.ShapeDtypeStruct((count, EDGE), jnp.float32)],
        compiler_params=pltpu.CompilerParams(vmem_limit_bytes=16 * 2**20),
        cost_estimate=pl.CostEstimate(
            flops=0, bytes_accessed=6 * int(np.prod(shape)), transcendentals=0
        ),
    )(window)


def match_kernel(step, me, even, odd, both, row_scale, *refs):
    pieces, (out, c_even, c_odd, c_both, done, sems) = refs[:4], refs[-6:]
    count, seg = pieces[0].shape[1:]
    width = c_even.shape[0]
    r, h = held(me[0], step)
    k = lax.rem(me[0] // XS, KS)
    for piece, at in zip(pieces, (h * 2 + k, 2 - h * 2 + k, h * 2 + 1 - k, 3 - h * 2 - k)):
        row = pl.ds(pl.multiple_of(at * count, count), count)
        for g in range(XS):
            for a in range(2):
                lanes = slice((2 * g + a) * EDGE, (2 * g + a + 1) * EDGE)
                c_even[row, lanes] = piece[g, :, 2 * a * EDGE : (2 * a + 1) * EDGE]
                c_odd[row, lanes] = piece[g, :, (2 * a + 1) * EDGE : (2 * a + 2) * EDGE]
    wide_even = c_even[...].astype(jnp.float32)
    wide_odd = c_odd[...].astype(jnp.float32)
    c_both[...] = (wide_even + wide_odd).astype(jnp.bfloat16)
    total = jnp.sum(wide_even * wide_even + wide_odd * wide_odd, axis=1, keepdims=True)
    norm = lax.rsqrt(total / (XS * seg) + 1e-06)
    scale = row_scale[:, :1] * jnp.broadcast_to(norm, (width, EDGE)).T[:1]

    def products(rows, steps, columns):
        tiles = [
            jnp.concatenate(
                [
                    rows[g, :, (HALF_LAG - u) * EDGE : (HALF_LAG - u + 2) * EDGE]
                    for g in range(XS)
                ],
                axis=1,
            )
            for u in steps
        ]
        found = lax.dot_general(
            jnp.concatenate(tiles, axis=0),
            columns[...],
            (((1,), (1,)), ((), ())),
            preferred_element_type=jnp.float32,
        )
        return {u: found[n * count : (n + 1) * count] for n, u in enumerate(steps)}

    b = {}
    copies = []
    lanes = pl.ds(pl.multiple_of(r * width, width), width)
    for n, block in enumerate(BLOCKS):
        a = products(even, block, c_even)
        ahead = range(block[0], min(block[-1] + 2, HALF_LAG + 1))
        b.update(products(odd, [u for u in ahead if u not in b], c_odd))
        s = products(both, [u for u in block if u < HALF_LAG], c_both)
        for u in block:
            done[2 * u] = ((a[u] + b[u]) * scale).astype(jnp.bfloat16)
            if u in s:
                done[2 * u + 1] = ((s[u] - a[u] - b[u + 1]) * scale).astype(jnp.bfloat16)
        lags = pl.ds(2 * block[0], min(2 * len(block), LAGS - 2 * block[0]))
        copy = pltpu.make_async_copy(done.at[lags], out.at[lags, :, lanes], sems.at[n])
        copy.start()
        copies.append(copy)
    for copy in copies:
        copy.wait()


def match(me, step, rows, row_scale, pieces, result, columns):
    count, seg = pieces[0].shape[1:]
    samples = seg * XS
    width = 4 * count
    before = [] if result is None else [result]
    return pl.pallas_call(
        functools.partial(match_kernel, step),
        in_specs=[SCALAR] + [INSIDE] * 8 + [ANYWHERE] * len(before),
        out_specs=ANYWHERE,
        out_shape=jax.ShapeDtypeStruct((LAGS, count, columns), jnp.bfloat16),
        scratch_shapes=[pltpu.VMEM((width, samples // 2), jnp.bfloat16)] * 3
        + [
            pltpu.VMEM((LAGS, count, width), jnp.bfloat16),
            pltpu.SemaphoreType.DMA((len(BLOCKS),)),
        ],
        input_output_aliases={9: 0} if before else {},
        compiler_params=pltpu.CompilerParams(vmem_limit_bytes=24 * 2**20),
        cost_estimate=pl.CostEstimate(
            flops=3 * (LAGS + 1) * count * width * samples // 2,
            bytes_accessed=2 * LAGS * count * width,
            transcendentals=0,
        ),
    )(me, *rows, row_scale, *pieces, *before)


def on_device(series):
    count = series.shape[0]
    me = (lax.axis_index("chan") * XS + lax.axis_index("seg")).reshape(1)
    left = send(series, along_x(1))
    right = send(series, along_x(-1))
    far = send(series, along_x(2))
    own, move = own_segment(series)
    window = whole_window(me, own, move, left, right, far)
    *rows, row_scale = shifts(window)
    mine = send(window, to_columns)
    mine, row_scale, *rows = lax.optimization_barrier((mine, row_scale, *rows))
    beside = send(mine, other_y)
    above = send(mine, along_z(-1))
    below = send(mine, along_z(1))
    result = None
    for step, (first, second) in enumerate(((mine, beside), (above, below))):
        pieces = (first, second, send(first, other_core), send(second, other_core))
        result = match(me, step, rows, row_scale, pieces, result, 8 * count)
    return result


def solution(mesh):
    placed = (P("chan", ("win", "seg")),)
    return jax.shard_map(
        on_device, mesh=mesh, in_specs=placed, out_specs=P("win", "chan", "seg"), check_vma=False
    )
```

time: 54.4 us -> 48.9 us (0.90)
  Pallas kernels: 15.1 us -> 11.9 us
  waiting for transfers between devices: 8.52 us -> 5.45 us
  starting transfers between devices: 29.7 us -> 30.3 us
    pallas_call x4 -> x5, Pallas kernels: 15.1 us -> 11.9 us  [the longest x2 9.25 us: match(): pl.pallas_call(functools.partial(match_kernel, step), in_specs=[SCALAR] +...]
    ppermute x11, waiting for transfers between devices: 8.52 us -> 5.45 us  [send(): return lax.ppermute(value, AXES, pairs(target))]
    ppermute x11, starting transfers between devices: 29.7 us -> 30.3 us  [send(): return lax.ppermute(value, AXES, pairs(target))]
  transfers between devices with their start and end apart: 11 -> 11, of which waited for: 3 -> 3; matrix products, arithmetic and copies ran while one was open for 0% -> 0% of each run, Pallas kernels for 15% -> 14%
where the time goes in v5:
time: 48.9 us; the launch traced here: 48.7 us
  starting transfers between devices  30.3 us (62%)
  Pallas kernels  11.9 us (24%)
  waiting for transfers between devices  5.45 us (11%)
  local copies, waits for them, and re-layouts  0.87 us (2%)
    ppermute x11, starting transfers between devices, send(): return lax.ppermute(value, AXES, pairs(target))  30.3 us
    pallas_call x2, Pallas kernels, match(): pl.pallas_call(functools.partial(match_kernel, step), in_specs=[SCALAR] +...  9.25 us
    ppermute x11, waiting for transfers between devices, send(): return lax.ppermute(value, AXES, pairs(target))  5.45 us
    pallas_call x1, Pallas kernels, shifts(): pl.pallas_call(shift_kernel, in_specs=[INSIDE], out_specs=[INSIDE] * 4, o...  1.84 us
  transfers between devices with their start and end apart: 11, of which 3 were waited for; matrix products, arithmetic and copies ran while one was open for 0% of the time, Pallas kernels for 14%

profile of v5, /device:TPU:1, one launch (start us, length us, event | category | flops | bytes accessed | tf_op | source)
XLA Modules:
  0.0 48.7 jit_solution(9782353818849824572)
XLA Ops:
  0.0 2.0 %collective-permute-start = (bf16[64,512]{1,0:T(8,128)(2,1)}, bf16[64,512]{1,0:T(8,128)(2,1)S(1)}, u32[]{:S(2)}, u32[]{:S(2)}) collective-permute-start(bf16[64,512]{1,0:T(8,128)(2,1)} %series.1), channel_id=1, source_target_pairs={{0,2},{1,3},{2,4},{3,5},{4,6},{5,7},{6,0},{7,1},{8,10},{9,11},{10,... | collective-permute-start | bytes 196616 | tf_op jit(solution)/shard_map/ppermute | solution.py:39
  2.0 2.5 %collective-permute-start.2 = (bf16[64,512]{1,0:T(8,128)(2,1)}, bf16[64,512]{1,0:T(8,128)(2,1)S(1)}, u32[]{:S(2)}, u32[]{:S(2)}) collective-permute-start(bf16[64,512]{1,0:T(8,128)(2,1)} %series.1), channel_id=1, source_target_pairs={{0,4},{1,5},{2,6},{3,7},{4,0},{5,1},{6,2},{7,3},{8,12},{9,13},{10,... | collective-permute-start | bytes 196616 | tf_op jit(solution)/shard_map/ppermute | solution.py:39
  4.5 1.2 %collective-permute-start.1 = (bf16[64,512]{1,0:T(8,128)(2,1)}, bf16[64,512]{1,0:T(8,128)(2,1)S(1)}, u32[]{:S(2)}, u32[]{:S(2)}) collective-permute-start(bf16[64,512]{1,0:T(8,128)(2,1)} %series.1), channel_id=1, source_target_pairs={{0,6},{1,7},{2,0},{3,1},{4,2},{5,3},{6,4},{7,5},{8,14},{9,15},{10,... | collective-permute-start | bytes 196616 | tf_op jit(solution)/shard_map/ppermute | solution.py:39
  5.6 0.0 copy-start
  5.6 0.9 %copy-done = bf16[64,512]{1,0:T(8,128)(2,1)S(1)} copy-done((bf16[64,512]{1,0:T(8,128)(2,1)S(1)}, bf16[64,512]{1,0:T(8,128)(2,1)}, u32[]{:S(2)}) %copy-start) | copy-done | bytes 65560
  6.5 0.4 shard_map.17
  6.9 0.0 collective-permute-done.left
  6.9 0.4 collective-permute-done.2.far
  7.3 0.8 %collective-permute-done.1.right = bf16[64,512]{1,0:T(8,128)(2,1)S(1)} collective-permute-done((bf16[64,512]{1,0:T(8,128)(2,1)}, bf16[64,512]{1,0:T(8,128)(2,1)S(1)}, u32[]{:S(2)}, u32[]{:S(2)}) %collective-permute-start.1) | collective-permute-done | bytes 65568 | tf_op jit(solution)/shard_map/ppermute | solution.py:39
  8.1 0.4 shard_map.18.window
  8.5 10.8 %collective-permute-start.3 = (bf16[4,64,512]{2,1,0:T(8,128)(2,1)S(1)}, bf16[4,64,512]{2,1,0:T(8,128)(2,1)S(1)}, u32[]{:S(2)}, u32[]{:S(2)}) collective-permute-start(bf16[4,64,512]{2,1,0:T(8,128)(2,1)S(1)} %shard_map.18.window), channel_id=1, source_target_pairs={{0,80},{1,81},{2,0},{3,1},{4,208},{5,209},{6,128},{7,129},{8,216},... | collective-permute-start | bytes 786440 | tf_op jit(solution)/shard_map/ppermute | solution.py:39
  19.3 1.8 %shard_map.19 = (bf16[4,64,4352]{2,1,0:T(8,128)(2,1)S(1)}, bf16[4,64,4352]{2,1,0:T(8,128)(2,1)S(1)}, bf16[4,64,4352]{2,1,0:T(8,128)(2,1)S(1)}, f32[64,128]{1,0:T(8,128)S(1)}) custom-call(bf16[4,64,512]{2,1,0:T(8,128)(2,1)S(1)} %shard_map.18.window), custom_call_target="tpu_custom_call" | custom-call | bytes 6684672 | tf_op jit(solution)/shard_map/pallas_call | solution.py:147
  21.2 4.3 %collective-permute-done.3.refs_0_ = bf16[4,64,512]{2,1,0:T(8,128)(2,1)S(1)} collective-permute-done((bf16[4,64,512]{2,1,0:T(8,128)(2,1)S(1)}, bf16[4,64,512]{2,1,0:T(8,128)(2,1)S(1)}, u32[]{:S(2)}, u32[]{:S(2)}) %collective-permute-start.3) | collective-permute-done | bytes 262176 | tf_op jit(solution)/shard_map/ppermute | solution.py:39
  25.4 0.1 collective-permute-start.8
  25.5 0.0 collective-permute-start.5
  25.5 4.2 %collective-permute-start.4 = (bf16[4,64,512]{2,1,0:T(8,128)(2,1)S(1)}, bf16[4,64,512]{2,1,0:T(8,128)(2,1)S(1)}, u32[]{:S(2)}, u32[]{:S(2)}) collective-permute-start(bf16[4,64,512]{2,1,0:T(8,128)(2,1)S(1)} %collective-permute-done.3.refs_0_), channel_id=1, source_target_pairs={{0,224},{1,225},{2,226},{3,227},{4,228},{5,229},{6,230},{7,231},{8... | collective-permute-start | bytes 786440 | tf_op jit(solution)/shard_map/ppermute | solution.py:39
  29.7 5.3 %collective-permute-start.9 = (bf16[4,64,512]{2,1,0:T(8,128)(2,1)S(1)}, bf16[4,64,512]{2,1,0:T(8,128)(2,1)S(1)}, u32[]{:S(2)}, u32[]{:S(2)}) collective-permute-start(bf16[4,64,512]{2,1,0:T(8,128)(2,1)S(1)} %collective-permute-done.3.refs_0_), channel_id=1, source_target_pairs={{0,8},{1,9},{2,10},{3,11},{4,12},{5,13},{6,14},{7,15},{8,0},{9,1},... | collective-permute-start | bytes 786440 | tf_op jit(solution)/shard_map/ppermute | solution.py:39
  34.9 0.0 collective-permute-done.8.refs_1_
  34.9 0.0 collective-permute-start.10
  34.9 0.0 collective-permute-done.5.refs_1_
  34.9 4.3 %collective-permute-start.7 = (bf16[4,64,512]{2,1,0:T(8,128)(2,1)S(1)}, bf16[4,64,512]{2,1,0:T(8,128)(2,1)S(1)}, u32[]{:S(2)}, u32[]{:S(2)}) collective-permute-start(bf16[4,64,512]{2,1,0:T(8,128)(2,1)S(1)} %collective-permute-done.5.refs_1_), channel_id=1, source_target_pairs={{0,8},{1,9},{2,10},{3,11},{4,12},{5,13},{6,14},{7,15},{8,0},{9,1},... | collective-permute-start | bytes 786440 | tf_op jit(solution)/shard_map/ppermute | solution.py:39
  39.3 0.0 collective-permute-done.4.refs_0_
  39.3 0.0 collective-permute-start.6
  39.3 0.0 collective-permute-done.9.refs_2_
  39.3 0.0 collective-permute-done.10.refs_3_
  39.3 4.6 %shard_map.20.refs_4_ = bf16[65,64,512]{2,1,0:T(8,128)(2,1)} custom-call(s32[1]{0:T(128)} %bitcast.me, bf16[4,64,4352]{2,1,0:T(8,128)(2,1)S(1)} %get-tuple-element.22.even, bf16[4,64,4352]{2,1,0:T(8,128)(2,1)S(1)} %get-tuple-element.23.odd, bf16[4,64,4352]{2,1,0:T(8,128)(2,1)S(1)} %get-tuple-element.24.both, f32[64,128]{1,0:T(8,128)S(1)} %get-tuple-element.25.row_scale, ...), custom_call_target="tpu_custom_call" | custom-call | flops 3321888768 | bytes 2129920 | tf_op jit(solution)/shard_map/pallas_call | solution.py:224
  43.9 0.0 collective-permute-done.7.refs_3_
  43.9 0.0 collective-permute-done.6.refs_2_
  44.0 4.6 %shard_map.21 = bf16[65,64,512]{2,1,0:T(8,128)(2,1)} custom-call(s32[1]{0:T(128)} %bitcast.me, bf16[4,64,4352]{2,1,0:T(8,128)(2,1)S(1)} %get-tuple-element.22.even, bf16[4,64,4352]{2,1,0:T(8,128)(2,1)S(1)} %get-tuple-element.23.odd, bf16[4,64,4352]{2,1,0:T(8,128)(2,1)S(1)} %get-tuple-element.24.both, ...), custom_call_target="tpu_custom_call", output_to_operand_aliasing={{}: (9, {})} | custom-call | flops 3321888768 | bytes 2129920 | tf_op jit(solution)/shard_map/pallas_call | solution.py:224
Async XLA Ops:
  0.0 6.9 %collective-permute-start = (bf16[64,512]{1,0:T(8,128)(2,1)}, bf16[64,512]{1,0:T(8,128)(2,1)S(1)}, u32[]{:S(2)}, u32[]{:S(2)}) collective-permute-start(bf16[64,512]{1,0:T(8,128)(2,1)} %series.1), channel_id=1, source_target_pairs={{0,2},{1,3},{2,4},{3,5},{4,6},{5,7},{6,0},{7,1},{8,10},{9,11},{10,... | collective-permute-start | bytes 196616 | tf_op jit(solution)/shard_map/ppermute | solution.py:39
  2.0 5.3 %collective-permute-start.2 = (bf16[64,512]{1,0:T(8,128)(2,1)}, bf16[64,512]{1,0:T(8,128)(2,1)S(1)}, u32[]{:S(2)}, u32[]{:S(2)}) collective-permute-start(bf16[64,512]{1,0:T(8,128)(2,1)} %series.1), channel_id=1, source_target_pairs={{0,4},{1,5},{2,6},{3,7},{4,0},{5,1},{6,2},{7,3},{8,12},{9,13},{10,... | collective-permute-start | bytes 196616 | tf_op jit(solution)/shard_map/ppermute | solution.py:39
  4.5 3.6 %collective-permute-start.1 = (bf16[64,512]{1,0:T(8,128)(2,1)}, bf16[64,512]{1,0:T(8,128)(2,1)S(1)}, u32[]{:S(2)}, u32[]{:S(2)}) collective-permute-start(bf16[64,512]{1,0:T(8,128)(2,1)} %series.1), channel_id=1, source_target_pairs={{0,6},{1,7},{2,0},{3,1},{4,2},{5,3},{6,4},{7,5},{8,14},{9,15},{10,... | collective-permute-start | bytes 196616 | tf_op jit(solution)/shard_map/ppermute | solution.py:39
  5.6 0.9 %copy-start = (bf16[64,512]{1,0:T(8,128)(2,1)S(1)}, bf16[64,512]{1,0:T(8,128)(2,1)}, u32[]{:S(2)}) copy-start(bf16[64,512]{1,0:T(8,128)(2,1)} %series.1) | copy-start | bytes 196612
  8.5 16.9 %collective-permute-start.3 = (bf16[4,64,512]{2,1,0:T(8,128)(2,1)S(1)}, bf16[4,64,512]{2,1,0:T(8,128)(2,1)S(1)}, u32[]{:S(2)}, u32[]{:S(2)}) collective-permute-start(bf16[4,64,512]{2,1,0:T(8,128)(2,1)S(1)} %shard_map.18.window), channel_id=1, source_target_pairs={{0,80},{1,81},{2,0},{3,1},{4,208},{5,209},{6,128},{7,129},{8,216},... | collective-permute-start | bytes 786440 | tf_op jit(solution)/shard_map/ppermute | solution.py:39
  25.4 9.5 %collective-permute-start.8 = (bf16[4,64,512]{2,1,0:T(8,128)(2,1)S(1)}, bf16[4,64,512]{2,1,0:T(8,128)(2,1)S(1)}, u32[]{:S(2)}, u32[]{:S(2)}) collective-permute-start(bf16[4,64,512]{2,1,0:T(8,128)(2,1)S(1)} %collective-permute-done.3.refs_0_), channel_id=1, source_target_pairs={{0,16},{1,17},{2,18},{3,19},{4,20},{5,21},{6,22},{7,23},{8,24},{9,... | collective-permute-start | bytes 786440 | tf_op jit(solution)/shard_map/ppermute | solution.py:39
  25.5 9.5 %collective-permute-start.5 = (bf16[4,64,512]{2,1,0:T(8,128)(2,1)S(1)}, bf16[4,64,512]{2,1,0:T(8,128)(2,1)S(1)}, u32[]{:S(2)}, u32[]{:S(2)}) collective-permute-start(bf16[4,64,512]{2,1,0:T(8,128)(2,1)S(1)} %collective-permute-done.3.refs_0_), channel_id=1, source_target_pairs={{0,32},{1,33},{2,34},{3,35},{4,36},{5,37},{6,38},{7,39},{8,40},{9,... | collective-permute-start | bytes 786440 | tf_op jit(solution)/shard_map/ppermute | solution.py:39
  25.5 13.8 %collective-permute-start.4 = (bf16[4,64,512]{2,1,0:T(8,128)(2,1)S(1)}, bf16[4,64,512]{2,1,0:T(8,128)(2,1)S(1)}, u32[]{:S(2)}, u32[]{:S(2)}) collective-permute-start(bf16[4,64,512]{2,1,0:T(8,128)(2,1)S(1)} %collective-permute-done.3.refs_0_), channel_id=1, source_target_pairs={{0,224},{1,225},{2,226},{3,227},{4,228},{5,229},{6,230},{7,231},{8... | collective-permute-start | bytes 786440 | tf_op jit(solution)/shard_map/ppermute | solution.py:39
  29.7 9.6 %collective-permute-start.9 = (bf16[4,64,512]{2,1,0:T(8,128)(2,1)S(1)}, bf16[4,64,512]{2,1,0:T(8,128)(2,1)S(1)}, u32[]{:S(2)}, u32[]{:S(2)}) collective-permute-start(bf16[4,64,512]{2,1,0:T(8,128)(2,1)S(1)} %collective-permute-done.3.refs_0_), channel_id=1, source_target_pairs={{0,8},{1,9},{2,10},{3,11},{4,12},{5,13},{6,14},{7,15},{8,0},{9,1},... | collective-permute-start | bytes 786440 | tf_op jit(solution)/shard_map/ppermute | solution.py:39
  34.9 4.4 %collective-permute-start.10 = (bf16[4,64,512]{2,1,0:T(8,128)(2,1)S(1)}, bf16[4,64,512]{2,1,0:T(8,128)(2,1)S(1)}, u32[]{:S(2)}, u32[]{:S(2)}) collective-permute-start(bf16[4,64,512]{2,1,0:T(8,128)(2,1)S(1)} %collective-permute-done.8.refs_1_), channel_id=1, source_target_pairs={{0,8},{1,9},{2,10},{3,11},{4,12},{5,13},{6,14},{7,15},{8,0},{9,1},... | collective-permute-start | bytes 786440 | tf_op jit(solution)/shard_map/ppermute | solution.py:39
  34.9 9.0 %collective-permute-start.7 = (bf16[4,64,512]{2,1,0:T(8,128)(2,1)S(1)}, bf16[4,64,512]{2,1,0:T(8,128)(2,1)S(1)}, u32[]{:S(2)}, u32[]{:S(2)}) collective-permute-start(bf16[4,64,512]{2,1,0:T(8,128)(2,1)S(1)} %collective-permute-done.5.refs_1_), channel_id=1, source_target_pairs={{0,8},{1,9},{2,10},{3,11},{4,12},{5,13},{6,14},{7,15},{8,0},{9,1},... | collective-permute-start | bytes 786440 | tf_op jit(solution)/shard_map/ppermute | solution.py:39
  39.3 4.7 %collective-permute-start.6 = (bf16[4,64,512]{2,1,0:T(8,128)(2,1)S(1)}, bf16[4,64,512]{2,1,0:T(8,128)(2,1)S(1)}, u32[]{:S(2)}, u32[]{:S(2)}) collective-permute-start(bf16[4,64,512]{2,1,0:T(8,128)(2,1)S(1)} %collective-permute-done.4.refs_0_), channel_id=1, source_target_pairs={{0,8},{1,9},{2,10},{3,11},{4,12},{5,13},{6,14},{7,15},{8,0},{9,1},... | collective-permute-start | bytes 786440 | tf_op jit(solution)/shard_map/ppermute | solution.py:39

commit v6 on v5

--- a/solution.py
+++ b/solution.py
@@ -18,7 +18,7 @@
 PHASES = 4
 REACH = HALF_LAG // PHASES
 TILES = 2 * (2 * REACH + 1)
-BLOCKS = (range(0, 11), range(11, 22), range(22, HALF_LAG + 1))
+BLOCKS = (range(0, 13), range(13, 26), range(26, HALF_LAG + 1))
 INSIDE = pl.BlockSpec(memory_space=pltpu.VMEM)
 ANYWHERE = pl.BlockSpec(memory_space=pl.ANY)
 SCALAR = pl.BlockSpec(memory_space=pltpu.SMEM)
@@ -257,6 +257,7 @@
     below = send(mine, along_z(1))
     result = None
     for step, (first, second) in enumerate(((mine, beside), (above, below))):
+        first, second = lax.optimization_barrier((first, second))
         pieces = (first, second, send(first, other_core), send(second, other_core))
         result = match(me, step, rows, row_scale, pieces, result, 8 * count)
     return result

time: 48.9 us -> 48.7 us (level)
  waiting for transfers between devices: 5.45 us -> 8.68 us
  starting transfers between devices: 30.3 us -> 27.1 us
    ppermute x11, waiting for transfers between devices: 5.45 us -> 8.68 us  [send(): return lax.ppermute(value, AXES, pairs(target))]
    ppermute x11, starting transfers between devices: 30.3 us -> 27.1 us  [send(): return lax.ppermute(value, AXES, pairs(target))]
  transfers between devices with their start and end apart: 11 -> 11, of which waited for: 3 -> 5; matrix products, arithmetic and copies ran while one was open for 0% -> 0% of each run, Pallas kernels for 14% -> 14%
where the time goes in v6:
time: 48.7 us; the launch traced here: 48.6 us
  starting transfers between devices  27.1 us (56%)
  Pallas kernels  11.7 us (24%)
  waiting for transfers between devices  8.68 us (18%)
  local copies, waits for them, and re-layouts  0.87 us (2%)
    ppermute x11, starting transfers between devices, send(): return lax.ppermute(value, AXES, pairs(target))  27.1 us
    pallas_call x2, Pallas kernels, match(): pl.pallas_call(functools.partial(match_kernel, step), in_specs=[SCALAR] +...  9.08 us
    ppermute x11, waiting for transfers between devices, send(): return lax.ppermute(value, AXES, pairs(target))  8.68 us
    pallas_call x1, Pallas kernels, shifts(): pl.pallas_call(shift_kernel, in_specs=[INSIDE], out_specs=[INSIDE] * 4, o...  1.84 us
  transfers between devices with their start and end apart: 11, of which 5 were waited for; matrix products, arithmetic and copies ran while one was open for 0% of the time, Pallas kernels for 14%

profile of v6, /device:TPU:1, one launch (start us, length us, event | category | flops | bytes accessed | tf_op | source)
XLA Modules:
  0.0 48.6 jit_solution(3820747927027726159)
XLA Ops:
  0.0 2.0 %collective-permute-start = (bf16[64,512]{1,0:T(8,128)(2,1)}, bf16[64,512]{1,0:T(8,128)(2,1)S(1)}, u32[]{:S(2)}, u32[]{:S(2)}) collective-permute-start(bf16[64,512]{1,0:T(8,128)(2,1)} %series.1), channel_id=1, source_target_pairs={{0,2},{1,3},{2,4},{3,5},{4,6},{5,7},{6,0},{7,1},{8,10},{9,11},{10,... | collective-permute-start | bytes 196616 | tf_op jit(solution)/shard_map/ppermute | solution.py:39
  2.0 2.5 %collective-permute-start.2 = (bf16[64,512]{1,0:T(8,128)(2,1)}, bf16[64,512]{1,0:T(8,128)(2,1)S(1)}, u32[]{:S(2)}, u32[]{:S(2)}) collective-permute-start(bf16[64,512]{1,0:T(8,128)(2,1)} %series.1), channel_id=1, source_target_pairs={{0,4},{1,5},{2,6},{3,7},{4,0},{5,1},{6,2},{7,3},{8,12},{9,13},{10,... | collective-permute-start | bytes 196616 | tf_op jit(solution)/shard_map/ppermute | solution.py:39
  4.5 1.2 %collective-permute-start.1 = (bf16[64,512]{1,0:T(8,128)(2,1)}, bf16[64,512]{1,0:T(8,128)(2,1)S(1)}, u32[]{:S(2)}, u32[]{:S(2)}) collective-permute-start(bf16[64,512]{1,0:T(8,128)(2,1)} %series.1), channel_id=1, source_target_pairs={{0,6},{1,7},{2,0},{3,1},{4,2},{5,3},{6,4},{7,5},{8,14},{9,15},{10,... | collective-permute-start | bytes 196616 | tf_op jit(solution)/shard_map/ppermute | solution.py:39
  5.6 0.0 copy-start
  5.6 0.9 %copy-done = bf16[64,512]{1,0:T(8,128)(2,1)S(1)} copy-done((bf16[64,512]{1,0:T(8,128)(2,1)S(1)}, bf16[64,512]{1,0:T(8,128)(2,1)}, u32[]{:S(2)}) %copy-start) | copy-done | bytes 65560
  6.5 0.4 shard_map.17
  6.9 0.0 collective-permute-done.left
  6.9 0.4 collective-permute-done.2.far
  7.3 0.8 %collective-permute-done.1.right = bf16[64,512]{1,0:T(8,128)(2,1)S(1)} collective-permute-done((bf16[64,512]{1,0:T(8,128)(2,1)}, bf16[64,512]{1,0:T(8,128)(2,1)S(1)}, u32[]{:S(2)}, u32[]{:S(2)}) %collective-permute-start.1) | collective-permute-done | bytes 65568 | tf_op jit(solution)/shard_map/ppermute | solution.py:39
  8.1 0.4 shard_map.18.window
  8.5 10.8 %collective-permute-start.3 = (bf16[4,64,512]{2,1,0:T(8,128)(2,1)S(1)}, bf16[4,64,512]{2,1,0:T(8,128)(2,1)S(1)}, u32[]{:S(2)}, u32[]{:S(2)}) collective-permute-start(bf16[4,64,512]{2,1,0:T(8,128)(2,1)S(1)} %shard_map.18.window), channel_id=1, source_target_pairs={{0,80},{1,81},{2,0},{3,1},{4,208},{5,209},{6,128},{7,129},{8,216},... | collective-permute-start | bytes 786440 | tf_op jit(solution)/shard_map/ppermute | solution.py:39
  19.3 1.8 %shard_map.19 = (bf16[4,64,4352]{2,1,0:T(8,128)(2,1)S(1)}, bf16[4,64,4352]{2,1,0:T(8,128)(2,1)S(1)}, bf16[4,64,4352]{2,1,0:T(8,128)(2,1)S(1)}, f32[64,128]{1,0:T(8,128)S(1)}) custom-call(bf16[4,64,512]{2,1,0:T(8,128)(2,1)S(1)} %shard_map.18.window), custom_call_target="tpu_custom_call" | custom-call | bytes 6684672 | tf_op jit(solution)/shard_map/pallas_call | solution.py:147
  21.2 4.3 %collective-permute-done.3.refs_0_ = bf16[4,64,512]{2,1,0:T(8,128)(2,1)S(1)} collective-permute-done((bf16[4,64,512]{2,1,0:T(8,128)(2,1)S(1)}, bf16[4,64,512]{2,1,0:T(8,128)(2,1)S(1)}, u32[]{:S(2)}, u32[]{:S(2)}) %collective-permute-start.3) | collective-permute-done | bytes 262176 | tf_op jit(solution)/shard_map/ppermute | solution.py:39
  25.4 0.1 collective-permute-start.8
  25.5 0.0 collective-permute-start.5
  25.5 4.2 %collective-permute-start.4 = (bf16[4,64,512]{2,1,0:T(8,128)(2,1)S(1)}, bf16[4,64,512]{2,1,0:T(8,128)(2,1)S(1)}, u32[]{:S(2)}, u32[]{:S(2)}) collective-permute-start(bf16[4,64,512]{2,1,0:T(8,128)(2,1)S(1)} %collective-permute-done.3.refs_0_), channel_id=1, source_target_pairs={{0,224},{1,225},{2,226},{3,227},{4,228},{5,229},{6,230},{7,231},{8... | collective-permute-start | bytes 786440 | tf_op jit(solution)/shard_map/ppermute | solution.py:39
  29.7 3.2 %collective-permute-done.8.refs_1_ = bf16[4,64,512]{2,1,0:T(8,128)(2,1)S(1)} collective-permute-done((bf16[4,64,512]{2,1,0:T(8,128)(2,1)S(1)}, bf16[4,64,512]{2,1,0:T(8,128)(2,1)S(1)}, u32[]{:S(2)}, u32[]{:S(2)}) %collective-permute-start.8) | collective-permute-done | bytes 262176 | tf_op jit(solution)/shard_map/ppermute | solution.py:39
  32.8 2.1 %collective-permute-start.9 = (bf16[4,64,512]{2,1,0:T(8,128)(2,1)S(1)}, bf16[4,64,512]{2,1,0:T(8,128)(2,1)S(1)}, u32[]{:S(2)}, u32[]{:S(2)}) collective-permute-start(bf16[4,64,512]{2,1,0:T(8,128)(2,1)S(1)} %collective-permute-done.3.refs_0_), channel_id=1, source_target_pairs={{0,8},{1,9},{2,10},{3,11},{4,12},{5,13},{6,14},{7,15},{8,0},{9,1},... | collective-permute-start | bytes 786440 | tf_op jit(solution)/shard_map/ppermute | solution.py:39
  34.9 0.0 collective-permute-start.10
  34.9 0.0 collective-permute-done.5.refs_1_
  34.9 0.1 collective-permute-done.4.refs_0_
  35.0 4.3 %collective-permute-start.6 = (bf16[4,64,512]{2,1,0:T(8,128)(2,1)S(1)}, bf16[4,64,512]{2,1,0:T(8,128)(2,1)S(1)}, u32[]{:S(2)}, u32[]{:S(2)}) collective-permute-start(bf16[4,64,512]{2,1,0:T(8,128)(2,1)S(1)} %collective-permute-done.4.refs_0_), channel_id=1, source_target_pairs={{0,8},{1,9},{2,10},{3,11},{4,12},{5,13},{6,14},{7,15},{8,0},{9,1},... | collective-permute-start | bytes 786440 | tf_op jit(solution)/shard_map/ppermute | solution.py:39
  39.3 0.0 collective-permute-start.7
  39.3 0.0 collective-permute-done.9.refs_2_
  39.3 0.0 collective-permute-done.10.refs_3_
  39.3 4.5 %shard_map.20.refs_4_ = bf16[65,64,512]{2,1,0:T(8,128)(2,1)} custom-call(s32[1]{0:T(128)} %bitcast.me, bf16[4,64,4352]{2,1,0:T(8,128)(2,1)S(1)} %get-tuple-element.26.even, bf16[4,64,4352]{2,1,0:T(8,128)(2,1)S(1)} %get-tuple-element.27.odd, bf16[4,64,4352]{2,1,0:T(8,128)(2,1)S(1)} %get-tuple-element.28.both, f32[64,128]{1,0:T(8,128)S(1)} %get-tuple-element.29.row_scale, ...), custom_call_target="tpu_custom_call" | custom-call | flops 3321888768 | bytes 2129920 | tf_op jit(solution)/shard_map/pallas_call | solution.py:224
  43.8 0.0 collective-permute-done.6.refs_2_
  43.9 0.0 collective-permute-done.7.refs_3_
  43.9 4.5 %shard_map.21 = bf16[65,64,512]{2,1,0:T(8,128)(2,1)} custom-call(s32[1]{0:T(128)} %bitcast.me, bf16[4,64,4352]{2,1,0:T(8,128)(2,1)S(1)} %get-tuple-element.26.even, bf16[4,64,4352]{2,1,0:T(8,128)(2,1)S(1)} %get-tuple-element.27.odd, bf16[4,64,4352]{2,1,0:T(8,128)(2,1)S(1)} %get-tuple-element.28.both, ...), custom_call_target="tpu_custom_call", output_to_operand_aliasing={{}: (9, {})} | custom-call | flops 3321888768 | bytes 2129920 | tf_op jit(solution)/shard_map/pallas_call | solution.py:224
Async XLA Ops:
  0.0 6.9 %collective-permute-start = (bf16[64,512]{1,0:T(8,128)(2,1)}, bf16[64,512]{1,0:T(8,128)(2,1)S(1)}, u32[]{:S(2)}, u32[]{:S(2)}) collective-permute-start(bf16[64,512]{1,0:T(8,128)(2,1)} %series.1), channel_id=1, source_target_pairs={{0,2},{1,3},{2,4},{3,5},{4,6},{5,7},{6,0},{7,1},{8,10},{9,11},{10,... | collective-permute-start | bytes 196616 | tf_op jit(solution)/shard_map/ppermute | solution.py:39
  2.0 5.3 %collective-permute-start.2 = (bf16[64,512]{1,0:T(8,128)(2,1)}, bf16[64,512]{1,0:T(8,128)(2,1)S(1)}, u32[]{:S(2)}, u32[]{:S(2)}) collective-permute-start(bf16[64,512]{1,0:T(8,128)(2,1)} %series.1), channel_id=1, source_target_pairs={{0,4},{1,5},{2,6},{3,7},{4,0},{5,1},{6,2},{7,3},{8,12},{9,13},{10,... | collective-permute-start | bytes 196616 | tf_op jit(solution)/shard_map/ppermute | solution.py:39
  4.5 3.6 %collective-permute-start.1 = (bf16[64,512]{1,0:T(8,128)(2,1)}, bf16[64,512]{1,0:T(8,128)(2,1)S(1)}, u32[]{:S(2)}, u32[]{:S(2)}) collective-permute-start(bf16[64,512]{1,0:T(8,128)(2,1)} %series.1), channel_id=1, source_target_pairs={{0,6},{1,7},{2,0},{3,1},{4,2},{5,3},{6,4},{7,5},{8,14},{9,15},{10,... | collective-permute-start | bytes 196616 | tf_op jit(solution)/shard_map/ppermute | solution.py:39
  5.6 0.9 %copy-start = (bf16[64,512]{1,0:T(8,128)(2,1)S(1)}, bf16[64,512]{1,0:T(8,128)(2,1)}, u32[]{:S(2)}) copy-start(bf16[64,512]{1,0:T(8,128)(2,1)} %series.1) | copy-start | bytes 196612
  8.5 16.9 %collective-permute-start.3 = (bf16[4,64,512]{2,1,0:T(8,128)(2,1)S(1)}, bf16[4,64,512]{2,1,0:T(8,128)(2,1)S(1)}, u32[]{:S(2)}, u32[]{:S(2)}) collective-permute-start(bf16[4,64,512]{2,1,0:T(8,128)(2,1)S(1)} %shard_map.18.window), channel_id=1, source_target_pairs={{0,80},{1,81},{2,0},{3,1},{4,208},{5,209},{6,128},{7,129},{8,216},... | collective-permute-start | bytes 786440 | tf_op jit(solution)/shard_map/ppermute | solution.py:39
  25.4 7.4 %collective-permute-start.8 = (bf16[4,64,512]{2,1,0:T(8,128)(2,1)S(1)}, bf16[4,64,512]{2,1,0:T(8,128)(2,1)S(1)}, u32[]{:S(2)}, u32[]{:S(2)}) collective-permute-start(bf16[4,64,512]{2,1,0:T(8,128)(2,1)S(1)} %collective-permute-done.3.refs_0_), channel_id=1, source_target_pairs={{0,16},{1,17},{2,18},{3,19},{4,20},{5,21},{6,22},{7,23},{8,24},{9,... | collective-permute-start | bytes 786440 | tf_op jit(solution)/shard_map/ppermute | solution.py:39
  25.5 9.5 %collective-permute-start.5 = (bf16[4,64,512]{2,1,0:T(8,128)(2,1)S(1)}, bf16[4,64,512]{2,1,0:T(8,128)(2,1)S(1)}, u32[]{:S(2)}, u32[]{:S(2)}) collective-permute-start(bf16[4,64,512]{2,1,0:T(8,128)(2,1)S(1)} %collective-permute-done.3.refs_0_), channel_id=1, source_target_pairs={{0,32},{1,33},{2,34},{3,35},{4,36},{5,37},{6,38},{7,39},{8,40},{9,... | collective-permute-start | bytes 786440 | tf_op jit(solution)/shard_map/ppermute | solution.py:39
  25.5 9.5 %collective-permute-start.4 = (bf16[4,64,512]{2,1,0:T(8,128)(2,1)S(1)}, bf16[4,64,512]{2,1,0:T(8,128)(2,1)S(1)}, u32[]{:S(2)}, u32[]{:S(2)}) collective-permute-start(bf16[4,64,512]{2,1,0:T(8,128)(2,1)S(1)} %collective-permute-done.3.refs_0_), channel_id=1, source_target_pairs={{0,224},{1,225},{2,226},{3,227},{4,228},{5,229},{6,230},{7,231},{8... | collective-permute-start | bytes 786440 | tf_op jit(solution)/shard_map/ppermute | solution.py:39
  32.8 6.5 %collective-permute-start.9 = (bf16[4,64,512]{2,1,0:T(8,128)(2,1)S(1)}, bf16[4,64,512]{2,1,0:T(8,128)(2,1)S(1)}, u32[]{:S(2)}, u32[]{:S(2)}) collective-permute-start(bf16[4,64,512]{2,1,0:T(8,128)(2,1)S(1)} %collective-permute-done.3.refs_0_), channel_id=1, source_target_pairs={{0,8},{1,9},{2,10},{3,11},{4,12},{5,13},{6,14},{7,15},{8,0},{9,1},... | collective-permute-start | bytes 786440 | tf_op jit(solution)/shard_map/ppermute | solution.py:39
  34.9 4.4 %collective-permute-start.10 = (bf16[4,64,512]{2,1,0:T(8,128)(2,1)S(1)}, bf16[4,64,512]{2,1,0:T(8,128)(2,1)S(1)}, u32[]{:S(2)}, u32[]{:S(2)}) collective-permute-start(bf16[4,64,512]{2,1,0:T(8,128)(2,1)S(1)} %collective-permute-done.8.refs_1_), channel_id=1, source_target_pairs={{0,8},{1,9},{2,10},{3,11},{4,12},{5,13},{6,14},{7,15},{8,0},{9,1},... | collective-permute-start | bytes 786440 | tf_op jit(solution)/shard_map/ppermute | solution.py:39
  35.0 8.8 %collective-permute-start.6 = (bf16[4,64,512]{2,1,0:T(8,128)(2,1)S(1)}, bf16[4,64,512]{2,1,0:T(8,128)(2,1)S(1)}, u32[]{:S(2)}, u32[]{:S(2)}) collective-permute-start(bf16[4,64,512]{2,1,0:T(8,128)(2,1)S(1)} %collective-permute-done.4.refs_0_), channel_id=1, source_target_pairs={{0,8},{1,9},{2,10},{3,11},{4,12},{5,13},{6,14},{7,15},{8,0},{9,1},... | collective-permute-start | bytes 786440 | tf_op jit(solution)/shard_map/ppermute | solution.py:39
  39.3 4.6 %collective-permute-start.7 = (bf16[4,64,512]{2,1,0:T(8,128)(2,1)S(1)}, bf16[4,64,512]{2,1,0:T(8,128)(2,1)S(1)}, u32[]{:S(2)}, u32[]{:S(2)}) collective-permute-start(bf16[4,64,512]{2,1,0:T(8,128)(2,1)S(1)} %collective-permute-done.5.refs_1_), channel_id=1, source_target_pairs={{0,8},{1,9},{2,10},{3,11},{4,12},{5,13},{6,14},{7,15},{8,0},{9,1},... | collective-permute-start | bytes 786440 | tf_op jit(solution)/shard_map/ppermute | solution.py:39
